TPU v7x, 256 devices: a whole 4x4x8 slice. The times are simulated.
256 devices in a mesh: slab: 32 (over y, x, core), batch: 8 (over z).
Axes of the slice: x: 4, y: 4, z: 8, core: 2. Of those that a mesh axis runs over, the one named last changes fastest.
Arguments:
- volume: bfloat16 [384, 384, 768], P('slab', 'batch'), may hold values from -6 to 6
- images: bfloat16 [1024, 384, 768], P('slab', 'batch'), may hold values from -6 to 6
- orient_ids: int32 [1024], P('slab'), may hold values from 0 to 7
- defocus_ids: int32 [1024], P('slab'), may hold values from 0 to 7
- ctf_tables: bfloat16 [8, 384, 384], P(None, 'batch'), may hold values from -1 to 1
- tilt_z: int32 [8], replicated, may hold values from -256 to 256
- tilt_x: int32 [8], replicated, may hold values from 192 to 256
Outputs:
- density_map: float32 [2, 384, 384, 384], P(None, 'slab', 'batch')
Inputs may be any that keep to these rules, and one draw needn't show every extreme that they name: `orient_ids`: orientation of each particle, an index into tilt_z and tilt_x. `defocus_ids`: defocus class of each particle, an index into ctf_tables.
All inputs are finite; a program needn't handle non-finite values.
Results may differ from a plain program's by a relative error of at most 0.0012.
The roundings to bfloat16 on the way count: a program that leaves them out, or rounds other values in their place, can miss the bound.
Values may be sent and summed in bfloat16 or wider, within the bound.
A program may use at most 128 MiB of HBM per device.

v0:
```python
import math

import jax
import jax.numpy as jnp
from jax import lax
from jax.sharding import PartitionSpec as P

TAU = 1.0


def interp_table(tilts, offset, extent, box_len):
    centre = box_len // 2
    column = jnp.arange(box_len, dtype=jnp.int32)
    plane_ids = offset + jnp.arange(extent, dtype=jnp.int32)
    position = centre * 256 + (column[None, :] - centre) * tilts[:, None]
    low_plane = position // 256
    fraction = (position - low_plane * 256).astype(jnp.float32) / 256.0
    low_hit = plane_ids[None, :, None] == low_plane[:, None, :]
    high_hit = plane_ids[None, :, None] == low_plane[:, None, :] + 1
    weights = jnp.where(low_hit, 1.0 - fraction[:, None, :], 0.0) + jnp.where(
        high_hit, fraction[:, None, :], 0.0
    )
    return weights.astype(jnp.bfloat16)


def dft_tables(box_len):
    indices = jnp.arange(box_len, dtype=jnp.int32)
    phases = indices[:, None] * indices[None, :] % box_len
    angles = phases.astype(jnp.float32) * (2.0 * math.pi / box_len)
    factor = 1.0 / math.sqrt(box_len)
    return (
        (jnp.cos(angles) * factor).astype(jnp.bfloat16),
        (jnp.sin(angles) * factor).astype(jnp.bfloat16),
    )


def complex_pass(real_part, imag_part, cos_tab, sin_tab, form):
    out_real = jnp.einsum(
        form, real_part, cos_tab, preferred_element_type=jnp.float32
    ) - jnp.einsum(form, imag_part, sin_tab, preferred_element_type=jnp.float32)
    out_imag = jnp.einsum(
        form, real_part, sin_tab, preferred_element_type=jnp.float32
    ) + jnp.einsum(form, imag_part, cos_tab, preferred_element_type=jnp.float32)
    return (out_real, out_imag)


def local(volume, images, orient_ids, defocus_ids, ctf_tables, tilt_z, tilt_x):
    planes, rows_dev, width_two = volume.shape
    box_len = width_two // 2
    orients = tilt_z.shape[0]
    defoci = ctf_tables.shape[0]
    offset = lax.axis_index("slab") * planes
    depth_tab = interp_table(tilt_z, offset, planes, box_len)
    width_tab = interp_table(tilt_x, jnp.int32(0), box_len, box_len)
    volume_cube = volume.reshape(planes, rows_dev, 2, box_len)
    partial_list = []
    for orient in range(orients):
        resampled = jnp.einsum(
            "zycx,xk->zyck", volume_cube, width_tab[orient], preferred_element_type=jnp.float32
        )
        project_depth_f = depth_tab[orient].astype(jnp.float32)
        partial_list.append(jnp.sum(resampled * project_depth_f[:, None, None, :], axis=0))
    partials = jnp.stack(partial_list)
    count_dev = images.shape[0]
    pictures = images.reshape(count_dev, rows_dev, 2, box_len)
    orient_hot = (orient_ids[:, None] == jnp.arange(orients, dtype=jnp.int32)[None, :]).astype(
        jnp.float32
    )
    defocus_hot = (defocus_ids[:, None] == jnp.arange(defoci, dtype=jnp.int32)[None, :]).astype(
        jnp.float32
    )
    ctf_rows = jnp.einsum(
        "pd,dyk->pyk", defocus_hot, ctf_tables.astype(jnp.float32), precision=lax.Precision.HIGHEST
    )
    ctf_power = jnp.einsum(
        "po,pyk->oyk", orient_hot, ctf_rows * ctf_rows, precision=lax.Precision.HIGHEST
    )
    projection = lax.psum(partials, "slab")
    expanded = jnp.einsum("po,oyck->pyck", orient_hot, projection, precision=lax.Precision.HIGHEST)
    mismatch = pictures.astype(jnp.float32) - ctf_rows[:, :, None, :] * expanded
    numer_local = jnp.einsum(
        "po,pyck->oyck",
        orient_hot,
        ctf_rows[:, :, None, :] * mismatch,
        precision=lax.Precision.HIGHEST,
    )
    numer_sums, ctf_power = lax.psum((numer_local, ctf_power), "slab")
    state_pair = (
        jnp.zeros((planes, rows_dev, 2, box_len), jnp.float32),
        jnp.zeros((planes, rows_dev, box_len), jnp.float32),
    )
    for orient in range(orients):
        spread_numer_vol, spread_weight_vol = state_pair
        depth_f = depth_tab[orient].astype(jnp.float32)
        operand = (depth_f[:, None, None, :] * numer_sums[orient][None]).astype(jnp.bfloat16)
        spread_numer_vol = spread_numer_vol + jnp.einsum(
            "zyck,xk->zycx", operand, width_tab[orient], preferred_element_type=jnp.float32
        )
        weight_op = (depth_f[:, None, :] * ctf_power[orient][None]).astype(jnp.bfloat16)
        spread_weight_vol = spread_weight_vol + jnp.einsum(
            "zyk,xk->zyx", weight_op, width_tab[orient], preferred_element_type=jnp.float32
        )
        state_pair = (spread_numer_vol, spread_weight_vol)
    numer_vol, weight_vol = state_pair
    updated = (
        volume_cube.astype(jnp.float32) + numer_vol / (weight_vol[:, :, None, :] + TAU)
    ).astype(jnp.bfloat16)
    cos_tab, sin_tab = dft_tables(box_len)
    out_real, out_imag = complex_pass(
        updated[:, :, 0], updated[:, :, 1], cos_tab, sin_tab, "zyx,xn->zyn"
    )
    along_x = jnp.stack([out_real, out_imag], axis=2).astype(jnp.bfloat16)
    pieces = lax.all_to_all(along_x, "batch", split_axis=3, concat_axis=1, tiled=True)
    row_real, row_imag = complex_pass(
        pieces[:, :, 0], pieces[:, :, 1], cos_tab, sin_tab, "zyx,yn->znx"
    )
    along_y = jnp.stack([row_real, row_imag], axis=2).astype(jnp.bfloat16)
    pieces = lax.all_to_all(along_y, "slab", split_axis=1, concat_axis=0, tiled=True)
    depth_real, depth_imag = complex_pass(
        pieces[:, :, 0], pieces[:, :, 1], cos_tab, sin_tab, "zyx,zn->yxn"
    )
    return jnp.stack([depth_real, depth_imag], axis=0)


def solution(mesh):
    in_specs = (
        P("slab", "batch", None),
        P("slab", "batch", None),
        P("slab"),
        P("slab"),
        P(None, "batch", None),
        P(),
        P(),
    )
    out_specs = P(None, "slab", "batch", None)
    return jax.shard_map(local, mesh=mesh, in_specs=in_specs, out_specs=out_specs, check_vma=False)
```

profile of v0, /device:TPU:1, one launch (start us, length us, event | category | flops | bytes accessed | tf_op | source)
XLA Modules:
  0.0 444.1 jit_solution(11875283931819296232)
XLA Ops:
  8.4 2.9 add_convert_fusion
  31.3 4.6 %stack.68 = f32[8,48,2,384]{3,0,2,1:T(8,128)} concatenate(f32[1,48,2,384]{3,0,2,1:T(1,128)} %copy.154, f32[1,48,2,384]{3,0,2,1:T(1,128)} %copy.155, f32[1,48,2,384]{3,0,2,1:T(1,128)} %copy.156, f32[1,48,2,384]{3,0,2,1:T(1,128)} %copy.157, f32[1,48,2,384]{3,0,2,1:T(1,128)} %copy.158, f32[1,48,2,384]{3,0,2,1:T(1,128)} %copy.159, f32[1,48,2,384]{3,0,2,1:T(1,128)} %copy.160, ...), dimensions={0} | concatenate | bytes 2359296 | tf_op jit(solution)/shard_map/stack | solution.py:63
  36.0 4.4 reshape.332
  42.9 112.0 %all-reduce.4.cloned.1.call-done = f32[8,48,2,384]{3,0,2,1:T(8,128)} async-done(((f32[8,48,2,384]{3,0,2,1:T(8,128)}), f32[8,48,2,384]{3,0,2,1:T(8,128)}) %all-reduce.4.cloned.1.call-update) | async-done | bytes 1179664 | tf_op jit(solution)/shard_map/psum | solution.py:78
  154.9 3.5 fusion.172
  158.4 5.7 %fusion.1 = f32[8,48,2,384]{3,0,2,1:T(8,128)} fusion(f32[32,48,2,384]{3,2,1,0:T(2,128)S(1)} %copy-done.3, f32[32,48,2,384]{3,0,2,1:T(8,128)S(1)} %fusion.172, f32[32,48,384]{2,0,1:T(8,128)S(1)} %fusion.117, s32[32]{0:T(128)S(1)} %copy-done.23), kind=kOutput, calls=%fused_computation.2 | convolution fusion | flops 116785408 | bytes 12976256 | tf_op jit(solution)/shard_map/po,pyck->oyck/dot_general | solution.py:81
  164.1 116.3 %all-reduce.6.cloned.1.call-done = (f32[8,48,2,384]{3,0,2,1:T(8,128)}, f32[8,48,384]{2,0,1:T(8,128)}) async-done(((f32[8,48,2,384]{3,0,2,1:T(8,128)}, f32[8,48,384]{2,0,1:T(8,128)}), (f32[8,48,2,384]{3,0,2,1:T(8,128)}, f32[8,48,384]{2,0,1:T(8,128)})) %all-reduce.6.cloned.1.call-update) | async-done | bytes 1769488 | tf_op jit(solution)/shard_map/psum | solution.py:87
  280.4 5.9 %fusion.230 = (f32[1,48,2,384]{3,0,2,1:T(1,128)S(1)}, f32[1,48,2,384]{3,0,2,1:T(1,128)S(1)}, f32[1,48,2,384]{3,0,2,1:T(1,128)S(1)}, f32[1,48,2,384]{3,0,2,1:T(1,...) fusion(f32[8,48,2,384]{3,0,2,1:T(8,128)} %get-tuple-element.5), kind=kLoop, calls=%fused_computation.324 | loop fusion | bytes 2359296 | tf_op jit(solution)/shard_map/slice | solution.py:95
  297.4 2.5 fusion.83
  299.9 2.5 fusion.84
  302.4 2.7 fusion.20
  305.1 2.5 fusion.21
  307.7 2.2 copy.138
  309.9 4.0 reshape.369
  313.9 30.7 %all_to_all.36 = bf16[8,2,27648]{2,1,0:T(2,128)(2,1)} all-to-all(bf16[8,2,27648]{2,1,0:T(2,128)(2,1)S(1)} %reshape.369), channel_id=1, replica_groups=mesh['slab'=32,'batch'=8] {'batch'}, dimensions={0} | all-to-all | bytes 1769472 | tf_op jit(solution)/shard_map/all_to_all | solution.py:113
  344.6 9.5 %reshape.370 = bf16[384,12,2,48]{3,2,1,0:T(2,128)(2,1)S(1)} reshape(bf16[8,2,27648]{2,1,0:T(2,128)(2,1)} %all_to_all.36) | data formatting | bytes 1769472
  354.1 2.9 copy.238
  357.1 4.0 all_to_all.29
  361.2 2.5 fusion.120
  363.6 2.5 fusion.121
  366.1 2.5 fusion.122
  368.6 2.5 fusion.119
  371.4 2.2 copy.140
  373.6 3.2 reshape.371
  376.8 22.9 %all_to_all.37 = bf16[32,2,6912]{2,1,0:T(2,128)(2,1)} all-to-all(bf16[32,2,6912]{2,1,0:T(2,128)(2,1)S(1)} %reshape.371), channel_id=1, replica_groups=mesh['slab'=32,'batch'=8] {'slab'}, dimensions={0} | all-to-all | bytes 1769472 | tf_op jit(solution)/shard_map/all_to_all | solution.py:118
  399.7 9.4 %reshape.372 = bf16[384,12,2,48]{3,2,1,0:T(2,128)(2,1)S(1)} reshape(bf16[32,2,6912]{2,1,0:T(2,128)(2,1)} %all_to_all.37) | data formatting | bytes 1769472
  410.7 4.7 %fusion.229 = (bf16[384,12,1,48]{3,2,1,0:T(2,128)(2,1)S(1)}, bf16[384,12,1,48]{3,2,1,0:T(2,128)(2,1)}) fusion(bf16[384,12,2,48]{3,2,1,0:T(2,128)(2,1)S(1)} %bitcast.330), kind=kLoop, calls=%fused_computation.323 | loop fusion | bytes 1769472 | tf_op jit(solution)/shard_map/slice | solution.py:120
  415.4 5.7 %copy.179 = bf16[384,12,1,48]{0,3,1,2:T(8,128)(2,1)S(1)} copy(bf16[384,12,1,48]{3,2,1,0:T(2,128)(2,1)} %get-tuple-element.8) | data formatting | bytes 884736
  421.0 3.4 fusion.63
  424.4 3.4 fusion.65
  429.5 3.7 fusion.17
  433.2 2.5 fusion.16
  (113 shorter events, 40.1 us)
Async XLA Ops:
  6.5 33.9 %copy-start = (bf16[8,48,384]{2,1,0:T(8,128)(2,1)S(1)}, bf16[8,48,384]{2,1,0:T(8,128)(2,1)}, u32[]{:S(2)}) copy-start(bf16[8,48,384]{2,1,0:T(8,128)(2,1)} %param.11) | copy-start | bytes 884740
  6.5 4.8 %copy-start.5 = (bf16[12,48,768]{2,1,0:T(8,128)(2,1)S(1)}, bf16[12,48,768]{2,1,0:T(8,128)(2,1)}, u32[]{:S(2)}) copy-start(bf16[12,48,768]{2,1,0:T(8,128)(2,1)} %param.7) | copy-start | bytes 2654212
  6.5 148.3 %all-reduce.4.cloned.1.call-start = ((), (), s32[]{:S(2)}) async-start(), calls=%async_computation.2 | async-start | bytes 2359296 | tf_op jit(solution)/shard_map/psum | solution.py:78
  8.3 4.7 %copy-start.19 = (f32[12,384]{1,0:T(8,128)}, f32[12,384]{1,0:T(8,128)S(1)}, u32[]{:S(2)}) copy-start(f32[12,384]{1,0:T(8,128)S(1)} %get-tuple-element.33) | copy-start | bytes 55300
  8.3 5.5 %copy-start.17 = (f32[12,384]{1,0:T(8,128)}, f32[12,384]{1,0:T(8,128)S(1)}, u32[]{:S(2)}) copy-start(f32[12,384]{1,0:T(8,128)S(1)} %get-tuple-element.32) | copy-start | bytes 55300
  8.4 8.0 %copy-start.15 = (f32[12,384]{1,0:T(8,128)}, f32[12,384]{1,0:T(8,128)S(1)}, u32[]{:S(2)}) copy-start(f32[12,384]{1,0:T(8,128)S(1)} %get-tuple-element.31) | copy-start | bytes 55300
  8.4 10.4 %copy-start.13 = (f32[12,384]{1,0:T(8,128)}, f32[12,384]{1,0:T(8,128)S(1)}, u32[]{:S(2)}) copy-start(f32[12,384]{1,0:T(8,128)S(1)} %get-tuple-element.30) | copy-start | bytes 55300
  8.4 12.9 %copy-start.11 = (f32[12,384]{1,0:T(8,128)}, f32[12,384]{1,0:T(8,128)S(1)}, u32[]{:S(2)}) copy-start(f32[12,384]{1,0:T(8,128)S(1)} %get-tuple-element.29) | copy-start | bytes 55300
  8.4 15.4 %copy-start.9 = (f32[12,384]{1,0:T(8,128)}, f32[12,384]{1,0:T(8,128)S(1)}, u32[]{:S(2)}) copy-start(f32[12,384]{1,0:T(8,128)S(1)} %get-tuple-element.28) | copy-start | bytes 55300
  8.4 17.9 %copy-start.7 = (f32[12,384]{1,0:T(8,128)}, f32[12,384]{1,0:T(8,128)S(1)}, u32[]{:S(2)}) copy-start(f32[12,384]{1,0:T(8,128)S(1)} %get-tuple-element.27) | copy-start | bytes 55300
  8.4 20.4 %copy-start.21 = (f32[12,384]{1,0:T(8,128)}, f32[12,384]{1,0:T(8,128)S(1)}, u32[]{:S(2)}) copy-start(f32[12,384]{1,0:T(8,128)S(1)} %get-tuple-element.34) | copy-start | bytes 55300
  31.3 4.7 %copy-start.4 = (bf16[32,48,768]{2,1,0:T(8,128)(2,1)S(1)}, bf16[32,48,768]{2,1,0:T(8,128)(2,1)}, u32[]{:S(2)}) copy-start(bf16[32,48,768]{2,1,0:T(8,128)(2,1)} %param.8) | copy-start | bytes 7077892
  35.9 4.5 %copy-start.24 = (s32[32]{0:T(128)S(1)}, s32[32]{0:T(128)}, u32[]{:S(2)}) copy-start(s32[32]{0:T(128)} %param.10) | copy-start | bytes 388
  35.9 244.4 %all-reduce.6.cloned.1.call-start = ((), (), s32[]{:S(2)}) async-start(), calls=%async_computation.3 | async-start | bytes 3538944 | tf_op jit(solution)/shard_map/psum | solution.py:87
  40.5 0.7 copy-start.23
  154.9 3.5 copy-start.3
  280.4 6.0 %copy-start.6 = (f32[8,48,384]{2,0,1:T(8,128)S(1)}, f32[8,48,384]{2,0,1:T(8,128)}, u32[]{:S(2)}) copy-start(f32[8,48,384]{2,0,1:T(8,128)} %get-tuple-element.6) | copy-start | bytes 1769476
  280.4 6.4 %copy-start.2 = (bf16[8,384,384]{2,1,0:T(8,128)(2,1)S(1)}, bf16[8,384,384]{2,1,0:T(8,128)(2,1)}, u32[]{:S(2)}) copy-start(bf16[8,384,384]{2,1,0:T(8,128)(2,1)} %add_convert_fusion) | copy-start | bytes 7077892
  280.4 6.4 %copy-start.22 = (f32[12,384]{1,0:T(8,128)S(1)}, f32[12,384]{1,0:T(8,128)}, u32[]{:S(2)}) copy-start(f32[12,384]{1,0:T(8,128)} %copy-done.21) | copy-start | bytes 55300
  286.3 0.9 copy-start.10
  287.2 0.8 copy-start.12
  288.0 0.8 copy-start.14
  288.8 0.8 copy-start.16
  289.5 1.0 copy-start.18
  290.5 0.8 copy-start.20
  294.6 0.9 copy-start.8
  429.4 3.7 copy-start.25
  433.2 3.8 copy-start.1
Sparse Core Ops, SparseCore 0:
  36.0 118.8 all-reduce.3
  164.2 116.0 all-reduce.5
where the time goes:
time: 452 us; the launch traced here: 444 us
  waiting for transfers between devices  228 us (50%)
  local copies, waits for them, and re-layouts  73.3 us (16%)
  matrix products  68.1 us (15%)
  blocking collectives  53.6 us (12%)
  between operations  14.4 us (3%)
  other arithmetic  6.39 us (1%)
    psum x1, waiting for transfers between devices, local(): numer_sums, ctf_power = lax.psum((numer_local, ctf_power), 'slab')  116 us
    psum x1, waiting for transfers between devices, local(): projection = lax.psum(partials, 'slab')  112 us
    unnamed x62, local copies, waits for them, and re-layouts  33.6 us
    all_to_all x1, blocking collectives, local(): lax.all_to_all(along_x, 'batch', split_axis=3, concat_axis=1, tiled=True)  30.7 us
    all_to_all x1, blocking collectives, local(): lax.all_to_all(along_y, 'slab', split_axis=1, concat_axis=0, tiled=True)  22.9 us
    dot_general x8, matrix products, local(): jnp.einsum('zycx,xk->zyck', volume_cube, width_tab[orient], preferred_ele...  13.4 us
    another operation x9, local copies, waits for them, and re-layouts, local(): partials = jnp.stack(partial_list)  11.1 us
    unnamed x4, matrix products  9.89 us
  transfers between devices with their start and end apart: 2, of which 2 were waited for; matrix products, arithmetic and copies ran while one was open for 2% of the time, Pallas kernels for 0%

commit v1 on v0

v1 whole, which is shorter than its diff:
```python
import functools
import math

import jax
import jax.numpy as jnp
import numpy as np
from jax import lax
from jax.experimental import pallas as pl
from jax.experimental.pallas import tpu as pltpu
from jax.sharding import PartitionSpec as P

TAU = 1.0
BOX = 384
HALF = 192
ORI = 8
DEF = 8
NS = 32
NB = 8
ZL = BOX // NS
YL = BOX // NB
XL = BOX // NB
CH = 3
ZC = ZL // CH
PIECE = 24
CHIPS = NS // 2
LANES = 640
F32 = jnp.float32
BF16 = jnp.bfloat16
VMEM = pl.BlockSpec(memory_space=pltpu.VMEM)
SMEM = pl.BlockSpec(memory_space=pltpu.SMEM)
LIMIT = 50 * 1024 * 1024


def dft_tables():
    index = np.arange(BOX, dtype=np.int64)
    phases = (index[:, None] * index[None, :] % BOX).astype(np.float64)
    angles = phases * (2.0 * math.pi / BOX)
    factor = 1.0 / math.sqrt(BOX)
    return np.cos(angles) * factor, np.sin(angles) * factor


def pass_tables():
    cos, sin = dft_tables()
    x_tab = np.concatenate([cos, -sin], axis=0).T
    full = np.stack([np.stack([cos, sin], 1), np.stack([-sin, cos], 1)], 0)
    y_tab = full.reshape(2, NB, YL, 2, NS, ZL).transpose(4, 3, 5, 1, 0, 2).reshape(2 * BOX, 2 * BOX)
    z_tab = full.reshape(2, NS, ZL, 2, BOX).transpose(2, 0, 1, 3, 4).reshape(2 * BOX, 2 * BOX)
    return tuple(jnp.asarray(t.astype(np.float32), F32).astype(BF16) for t in (x_tab, y_tab, z_tab))


def sums_kernel(orient_ref, defocus_ref, image_ref, ctf_ref, sum_ref, count_ref):
    sum_ref[...] = jnp.zeros_like(sum_ref)
    row = lax.broadcasted_iota(jnp.int32, count_ref.shape, 0)
    lane = lax.broadcasted_iota(jnp.int32, count_ref.shape, 1)

    def step(p, count):
        orient, defocus = orient_ref[p], defocus_ref[p]
        ctf = ctf_ref[defocus].astype(F32)
        for h in range(2):
            cols = slice(h * BOX, (h + 1) * BOX)
            sum_ref[orient, :, cols] += ctf * image_ref[p, :, cols].astype(F32)
        return count + jnp.where((row == orient) & (lane == defocus), 1.0, 0.0)

    count_ref[...] = lax.fori_loop(0, image_ref.shape[0], step, jnp.zeros(count_ref.shape, F32))


def local_sums(orient_ids, defocus_ids, images, ctf_tables):
    return pl.pallas_call(
        sums_kernel,
        out_shape=(
            jax.ShapeDtypeStruct((ORI, YL, 2 * BOX), F32),
            jax.ShapeDtypeStruct((8, 128), F32),
        ),
        in_specs=[SMEM, SMEM, VMEM, VMEM],
        out_specs=(VMEM, VMEM),
        compiler_params=pltpu.CompilerParams(vmem_limit_bytes=LIMIT),
        name="local_sums",
    )(orient_ids, defocus_ids, images, ctf_tables)


def slab_copy(src, dst, send, recv, to):
    return pltpu.make_async_remote_copy(
        src_ref=src, dst_ref=dst, send_sem=send, recv_sem=recv,
        device_id={"slab": to}, device_id_type=pl.DeviceIdType.MESH,
    )


def reduce_kernel(
    sum_ref, count_ref, edge_ref,
    out_ref, counts_ref, halo_ref,
    pair_buf, piece_buf, part_buf, total_buf, count_buf, count_pair,
    pair_send, pair_recv, part_send, part_recv, gather_send, gather_recv, twin_send, twin_recv,
    count_send, count_recv, halo_send, halo_recv,
):
    me = lax.axis_index("slab")
    core = lax.rem(me, 2)
    chip = me // 2
    twin = me + 1 - 2 * core
    below = lax.rem(me + NS - 1, NS)
    above = lax.rem(me + 1, NS)
    outer = lax.rem(me + NS + 2 * core - 1, NS)

    def peer(d):
        return 2 * lax.rem(chip + d, CHIPS) + core

    barrier = pltpu.get_barrier_semaphore()
    pl.semaphore_signal(barrier, inc=1, device_id={"slab": twin}, device_id_type=pl.DeviceIdType.MESH)
    pl.semaphore_signal(barrier, inc=1, device_id={"slab": outer}, device_id_type=pl.DeviceIdType.MESH)

    def greet(d, _):
        pl.semaphore_signal(barrier, inc=1, device_id={"slab": peer(d)}, device_id_type=pl.DeviceIdType.MESH)
        return 0

    lax.fori_loop(1, CHIPS, greet, 0)
    pl.semaphore_wait(barrier, CHIPS + 1)

    rows = ORI * YL // 2
    keep = pl.multiple_of(rows * core, rows)
    give = pl.multiple_of(rows * (1 - core), rows)
    pair = slab_copy(sum_ref.at[pl.ds(give, rows)], pair_buf, pair_send, pair_recv, twin)
    pair.start()
    count_twin = slab_copy(count_ref, count_pair, count_send.at[0], count_recv.at[0], twin)
    count_twin.start()
    halo_up = slab_copy(edge_ref.at[1], halo_ref.at[0], halo_send.at[0], halo_recv.at[0], above)
    halo_up.start()
    halo_down = slab_copy(edge_ref.at[0], halo_ref.at[1], halo_send.at[1], halo_recv.at[1], below)
    halo_down.start()

    count_twin.wait()
    count_buf[0] = count_ref[...] + count_pair[...]

    def count_go(d, _):
        slab_copy(count_buf.at[0], count_buf.at[d], count_send.at[d], count_recv.at[d], peer(d)).start()
        return 0

    lax.fori_loop(1, CHIPS, count_go, 0)

    pair.wait()
    for j in range(CHIPS):
        r, c = PIECE * (j // 2), BOX * (j % 2)
        piece_buf[j] = (
            sum_ref[pl.ds(pl.multiple_of(keep + r, 8), PIECE), c : c + BOX] + pair_buf[r : r + PIECE, c : c + BOX]
        )

    def part_copy(d):
        to = lax.rem(chip + d, CHIPS)
        return slab_copy(piece_buf.at[to], part_buf.at[d], part_send.at[d], part_recv.at[d], peer(d))

    def part_go(d, _):
        part_copy(d).start()
        return 0

    lax.fori_loop(1, CHIPS, part_go, 0)

    def part_add(d, _):
        part_copy(d).wait()
        total_buf[...] += part_buf[d]
        return 0

    total_buf[...] = piece_buf[chip]
    lax.fori_loop(1, CHIPS, part_add, 0)

    def place(ref, which):
        r = pl.multiple_of(keep + PIECE * (which // 2), 8)
        c = pl.multiple_of(BOX * lax.rem(which, 2), 128)
        return ref.at[pl.ds(r, PIECE), pl.ds(c, BOX)]

    def gather_copy(d):
        return slab_copy(total_buf, place(out_ref, chip), gather_send.at[d], gather_recv.at[d], peer(d))

    def gather_go(d, _):
        gather_copy(d).start()
        return 0

    lax.fori_loop(1, CHIPS, gather_go, 0)
    own_r = pl.multiple_of(keep + PIECE * (chip // 2), 8)
    own_c = pl.multiple_of(BOX * lax.rem(chip, 2), 128)
    out_ref[pl.ds(own_r, PIECE), pl.ds(own_c, BOX)] = total_buf[...]

    def twin_copy(d):
        which = lax.rem(chip + CHIPS - d, CHIPS)
        return slab_copy(place(out_ref, which), place(out_ref, which), twin_send.at[d], twin_recv.at[d], twin)

    twin_copy(0).start()

    def gather_done(d, _):
        gather_copy(d).wait()
        twin_copy(d).start()
        return 0

    lax.fori_loop(1, CHIPS, gather_done, 0)

    def count_done(d, total):
        slab_copy(count_buf.at[0], count_buf.at[d], count_send.at[d], count_recv.at[d], peer(d)).wait()
        return total + count_buf[d]

    counts_ref[...] = lax.fori_loop(1, CHIPS, count_done, count_buf[0])
    halo_up.wait()
    halo_down.wait()

    def twin_done(d, _):
        twin_copy(d).wait()
        return 0

    lax.fori_loop(0, CHIPS, twin_done, 0)


def reduce_sums(sums, counts, edges):
    dma = pltpu.SemaphoreType.DMA
    return pl.pallas_call(
        reduce_kernel,
        out_shape=(
            jax.ShapeDtypeStruct((ORI * YL, 2 * BOX), F32),
            jax.ShapeDtypeStruct((8, 128), F32),
            jax.ShapeDtypeStruct((2, YL, 2 * BOX), BF16),
        ),
        in_specs=[VMEM] * 3,
        out_specs=(VMEM,) * 3,
        scratch_shapes=[
            pltpu.VMEM((ORI * YL // 2, 2 * BOX), F32),
            pltpu.VMEM((CHIPS, PIECE, BOX), F32),
            pltpu.VMEM((CHIPS, PIECE, BOX), F32),
            pltpu.VMEM((PIECE, BOX), F32),
            pltpu.VMEM((CHIPS, 8, 128), F32),
            pltpu.VMEM((8, 128), F32),
            dma(()), dma(()),
            dma((CHIPS,)), dma((CHIPS,)), dma((CHIPS,)), dma((CHIPS,)), dma((CHIPS,)), dma((CHIPS,)),
            dma((CHIPS,)), dma((CHIPS,)), dma((2,)), dma((2,)),
        ],
        compiler_params=pltpu.CompilerParams(vmem_limit_bytes=LIMIT, collective_id=0, has_side_effects=True),
        name="reduce_sums",
    )(sums, counts, edges)


def interp_row(tilt):
    column = lax.broadcasted_iota(jnp.int32, (1, BOX), 1)
    position = HALF * 256 + (column - HALF) * tilt
    low = position >> 8
    fraction = (position & 255).astype(F32) * (1.0 / 256.0)
    return low, fraction


def update_kernel(
    sum_ref, count_ref, halo_ref, vol_ref, ctf_ref, tz_ref, tx_ref, xtab_ref,
    out_ref,
    width, depth, numer, power, operand, paired,
):
    first = lax.axis_index("slab") * ZL - 1
    plane = lax.broadcasted_iota(jnp.int32, (16, BOX), 0) + first
    column = lax.broadcasted_iota(jnp.int32, (BOX, BOX), 0)
    for o in range(ORI):
        low, frac = interp_row(tz_ref[o])
        weights = jnp.where(plane == low, 1.0 - frac, 0.0) + jnp.where(plane == low + 1, frac, 0.0)
        depth[o] = jnp.where(plane < BOX, weights, 0.0)
        low, frac = interp_row(tx_ref[o])
        table = jnp.where(column == low, 1.0 - frac, 0.0) + jnp.where(column == low + 1, frac, 0.0)
        width[:, o * BOX : (o + 1) * BOX] = table.astype(BF16)
    ctf = ctf_ref[...].astype(F32)
    square = ctf * ctf
    for o in range(ORI):
        total = jnp.zeros((YL, BOX), F32)
        for d in range(DEF):
            total = total + count_ref[o : o + 1, d : d + 1] * square[d]
        power[o] = total
        for h in range(2):
            cols = slice(h * BOX, (h + 1) * BOX)
            stack = jnp.concatenate(
                [halo_ref[0, :, cols][None], vol_ref[:, :, cols], halo_ref[1, :, cols][None]], axis=0
            ).reshape((ZL + 2) * YL, BOX)
            seen = jnp.dot(stack, width[:, o * BOX : (o + 1) * BOX], preferred_element_type=F32)
            seen = seen.reshape(ZL + 2, YL, BOX)
            proj = jnp.zeros((YL, BOX), F32)
            for j in range(ZL + 2):
                proj = proj + depth[o, j : j + 1, :] * seen[j]
            numer[o, :, cols] = sum_ref[o * YL : (o + 1) * YL, cols] - total * proj
    for c in range(CH):
        for o in range(ORI):
            k = slice(o * BOX, (o + 1) * BOX)
            for zi in range(ZC):
                j = c * ZC + zi + 1
                w = depth[o, j : j + 1, :]
                for h in range(2):
                    r = (zi * 2 + h) * YL
                    operand[r : r + YL, k] = (w * numer[o, :, h * BOX : (h + 1) * BOX]).astype(BF16)
                r = (2 * ZC + zi) * YL
                operand[r : r + YL, k] = (w * power[o]).astype(BF16)
        back = lax.dot_general(
            operand[...], width[...], (((1,), (1,)), ((), ())), preferred_element_type=F32
        )
        for zi in range(ZC):
            weight = back[(2 * ZC + zi) * YL : (2 * ZC + zi + 1) * YL] + TAU
            parts = []
            for h in range(2):
                r = (zi * 2 + h) * YL
                old = vol_ref[c * ZC + zi, :, h * BOX : (h + 1) * BOX].astype(F32)
                parts.append((old + back[r : r + YL] / weight).astype(BF16))
            r = zi * 2 * YL
            paired[r : r + YL, :BOX] = parts[0]
            paired[r : r + YL, BOX:] = parts[1]
            paired[r + YL : r + 2 * YL, :BOX] = parts[1]
            paired[r + YL : r + 2 * YL, BOX:] = -parts[0]
        out_ref[c] = lax.dot_general(
            xtab_ref[...], paired[...], (((1,), (1,)), ((), ())), preferred_element_type=F32
        ).astype(BF16)


def update_volume(sums, counts, halo, volume, ctf_tables, tilt_z, tilt_x, x_tab):
    return pl.pallas_call(
        update_kernel,
        out_shape=jax.ShapeDtypeStruct((CH, BOX, ZC * 2 * YL), BF16),
        in_specs=[VMEM] * 5 + [SMEM] * 2 + [VMEM],
        out_specs=VMEM,
        scratch_shapes=[
            pltpu.VMEM((BOX, ORI * BOX), BF16),
            pltpu.VMEM((ORI, 16, BOX), F32),
            pltpu.VMEM((ORI, YL, 2 * BOX), F32),
            pltpu.VMEM((ORI, YL, BOX), F32),
            pltpu.VMEM((ZC * 3 * YL, ORI * BOX), BF16),
            pltpu.VMEM((ZC * 2 * YL, 2 * BOX), BF16),
        ],
        compiler_params=pltpu.CompilerParams(vmem_limit_bytes=LIMIT),
        name="update_volume",
    )(sums, counts, halo, volume, ctf_tables, tilt_z, tilt_x, x_tab)


def batch_kernel(in_ref, out_ref, send, recv, own):
    me = lax.axis_index("batch")

    def peer(d):
        return lax.rem(me + d, NB)

    barrier = pltpu.get_barrier_semaphore()
    for d in range(1, NB):
        pl.semaphore_signal(barrier, inc=1, device_id={"batch": peer(d)}, device_id_type=pl.DeviceIdType.MESH)
    pl.semaphore_wait(barrier, NB - 1)

    def copy(c, d):
        return pltpu.make_async_remote_copy(
            src_ref=in_ref.at[c, peer(d)], dst_ref=out_ref.at[c, me], send_sem=send.at[c, d], recv_sem=recv.at[c, d],
            device_id={"batch": peer(d)}, device_id_type=pl.DeviceIdType.MESH,
        )

    local = [pltpu.make_async_copy(in_ref.at[c, me], out_ref.at[c, me], own.at[c]) for c in range(CH)]
    for c in range(CH):
        for d in (4, 3, 5, 2, 6, 1, 7):
            copy(c, d).start()
        local[c].start()
    for c in range(CH):
        for d in range(1, NB):
            copy(c, d).wait()
        local[c].wait()


def batch_exchange(x):
    dma = pltpu.SemaphoreType.DMA
    return pl.pallas_call(
        batch_kernel,
        out_shape=jax.ShapeDtypeStruct(x.shape, x.dtype),
        in_specs=[VMEM],
        out_specs=VMEM,
        scratch_shapes=[dma((CH, NB)), dma((CH, NB)), dma((CH,))],
        compiler_params=pltpu.CompilerParams(vmem_limit_bytes=LIMIT, collective_id=1, has_side_effects=True),
        name="batch_exchange",
    )(x)


def ypass_kernel(in_ref, ytab_ref, out_ref, gathered):
    for z in range(ZL):
        lanes = slice((z % ZC) * 2 * YL, (z % ZC + 1) * 2 * YL)
        gathered[z * XL : (z + 1) * XL, :] = jnp.concatenate(
            [in_ref[z // ZC, b, :, lanes] for b in range(NB)], axis=1
        )
    out = lax.dot_general(ytab_ref[...], gathered[...], (((1,), (1,)), ((), ())), preferred_element_type=F32)
    out_ref[:, :, : ZL * XL] = out.astype(BF16).reshape(NS, 2 * ZL, ZL * XL)
    out_ref[:, :, ZL * XL :] = jnp.zeros((NS, 2 * ZL, LANES - ZL * XL), BF16)


def ypass(x, y_tab):
    return pl.pallas_call(
        ypass_kernel,
        out_shape=jax.ShapeDtypeStruct((NS, 2 * ZL, LANES), BF16),
        in_specs=[VMEM, VMEM],
        out_specs=VMEM,
        scratch_shapes=[pltpu.VMEM((ZL * XL, 2 * BOX), BF16)],
        compiler_params=pltpu.CompilerParams(vmem_limit_bytes=LIMIT),
        name="ypass",
    )(x, y_tab)


def slab_kernel(in_ref, out_ref, send, recv, own):
    me = lax.axis_index("slab")

    def peer(d):
        return lax.rem(me + d, NS)

    barrier = pltpu.get_barrier_semaphore()

    def greet(d, _):
        pl.semaphore_signal(barrier, inc=1, device_id={"slab": peer(d)}, device_id_type=pl.DeviceIdType.MESH)
        return 0

    lax.fori_loop(1, NS, greet, 0)
    pl.semaphore_wait(barrier, NS - 1)

    def copy(d):
        return slab_copy(in_ref.at[peer(d)], out_ref.at[me], send.at[d], recv.at[d], peer(d))

    def go(d, _):
        copy(d).start()
        return 0

    local = pltpu.make_async_copy(in_ref.at[me], out_ref.at[me], own)
    local.start()
    lax.fori_loop(1, NS, go, 0)

    def done(d, _):
        copy(d).wait()
        return 0

    lax.fori_loop(1, NS, done, 0)
    local.wait()


def slab_exchange(x):
    dma = pltpu.SemaphoreType.DMA
    return pl.pallas_call(
        slab_kernel,
        out_shape=jax.ShapeDtypeStruct(x.shape, x.dtype),
        in_specs=[VMEM],
        out_specs=VMEM,
        scratch_shapes=[dma((NS,)), dma((NS,)), dma(())],
        compiler_params=pltpu.CompilerParams(vmem_limit_bytes=LIMIT, collective_id=2, has_side_effects=True),
        name="slab_exchange",
    )(x)


def zpass_kernel(in_ref, ztab_ref, out_ref, wide, gathered):
    for t in range(LANES // 128):
        lanes = slice(t * 128, (t + 1) * 128)
        wide[t] = in_ref[:, :, lanes].astype(F32).reshape(NS * 2 * ZL, 128)
    for z in range(ZL):
        lane = z * XL
        t, off = lane // 128, lane % 128
        for h in range(2):
            blocks = []
            for y in range(ZL):
                rows = pl.ds(h * ZL + y, NS, 2 * ZL)
                if off + XL <= 128:
                    blocks.append(wide[t, rows, :][:, off : off + XL])
                else:
                    both = jnp.concatenate([wide[t, rows, :], wide[t + 1, rows, :]], axis=1)
                    blocks.append(both[:, off : off + XL])
            r = (z * 2 + h) * NS
            gathered[r : r + NS, :] = jnp.concatenate(blocks, axis=1).astype(BF16)
    out = lax.dot_general(gathered[...], ztab_ref[...], (((0,), (0,)), ((), ())), preferred_element_type=F32)
    out_ref[0] = out[:, :BOX]
    out_ref[1] = out[:, BOX:]


def zpass(x, z_tab):
    return pl.pallas_call(
        zpass_kernel,
        out_shape=jax.ShapeDtypeStruct((2, ZL * XL, BOX), F32),
        in_specs=[VMEM, VMEM],
        out_specs=VMEM,
        scratch_shapes=[
            pltpu.VMEM((LANES // 128, NS * 2 * ZL, 128), F32),
            pltpu.VMEM((2 * BOX, ZL * XL), BF16),
        ],
        compiler_params=pltpu.CompilerParams(vmem_limit_bytes=LIMIT),
        name="zpass",
    )(x, z_tab)


def local(volume, images, orient_ids, defocus_ids, ctf_tables, tilt_z, tilt_x):
    x_tab, y_tab, z_tab = pass_tables()
    sums, counts = local_sums(orient_ids, defocus_ids, images, ctf_tables)
    edges = jnp.stack([volume[0], volume[-1]])
    sums, counts, halo = reduce_sums(sums.reshape(ORI * YL, 2 * BOX), counts, edges)
    along_x = update_volume(sums, counts, halo, volume, ctf_tables, tilt_z, tilt_x, x_tab)
    pieces = batch_exchange(along_x.reshape(CH, NB, XL, ZC * 2 * YL))
    along_y = ypass(pieces, y_tab)
    pieces = slab_exchange(along_y)
    return zpass(pieces, z_tab).reshape(2, ZL, XL, BOX)


def solution(mesh):
    in_specs = (
        P("slab", "batch", None),
        P("slab", "batch", None),
        P("slab"),
        P("slab"),
        P(None, "batch", None),
        P(),
        P(),
    )
    out_specs = P(None, "slab", "batch", None)
    return jax.shard_map(local, mesh=mesh, in_specs=in_specs, out_specs=out_specs, check_vma=False)
```

time: 452 us -> 103 us (0.23); the launches traced: 444 us -> 103 us
  waiting for transfers between devices: 228 us -> 0 us
  Pallas kernels: 0 us -> 98.2 us
  local copies, waits for them, and re-layouts: 73.3 us -> 4.9 us
  matrix products: 68.1 us -> 0 us
  blocking collectives: 53.6 us -> 0 us
  between operations: 14.4 us -> 0.16 us
  other arithmetic: 6.39 us -> 0.02 us
    psum x2 -> x0, waiting for transfers between devices: 228 us -> none  [the longest x1 116 us: local(): numer_sums, ctf_power = lax.psum((numer_local, ctf_power), 'slab')]
    pallas_call x0 -> x7, Pallas kernels: none -> 98.2 us  [the longest x1 30.6 us: reduce_sums(): pl.pallas_call(reduce_kernel, out_shape=(jax.ShapeDtypeStruct((ORI * YL,...]
    dot_general x36 -> x0, matrix products: 58.2 us -> none  [the longest x8 13.4 us: local(): jnp.einsum('zycx,xk->zyck', volume_cube, width_tab[orient], preferred_ele...]
    all_to_all x2 -> x0, blocking collectives: 53.6 us -> none  [the longest x1 30.7 us: local(): lax.all_to_all(along_x, 'batch', split_axis=3, concat_axis=1, tiled=True)]
    unnamed x62 -> x22, local copies, waits for them, and re-layouts: 33.6 us -> 3.97 us
    another operation x11 -> x0, local copies, waits for them, and re-layouts: 15.5 us -> none  [the longest x9 11.1 us: local(): partials = jnp.stack(partial_list)]
    slice x4 -> x1, local copies, waits for them, and re-layouts: 11.1 us -> 0.93 us  [local(): edges = jnp.stack([volume[0], volume[-1]])]
    unnamed x4 -> x0, matrix products: 9.89 us -> none
  transfers between devices with their start and end apart: 2 -> 0, of which waited for: 2 -> 0; matrix products, arithmetic and copies ran while one was open for 2% -> 0% of each run, Pallas kernels for 0% -> 0%
where the time goes in v1:
time: 103 us
  Pallas kernels  98.2 us (95%)
  local copies, waits for them, and re-layouts  4.9 us (5%)
    pallas_call x1, Pallas kernels, reduce_sums(): pl.pallas_call(reduce_kernel, out_shape=(jax.ShapeDtypeStruct((ORI * YL,...  30.6 us
    pallas_call x1, Pallas kernels, batch_exchange(): pl.pallas_call(batch_kernel, out_shape=jax.ShapeDtypeStruct(x.shape, x.dt...  28.2 us
    pallas_call x1, Pallas kernels, slab_exchange(): pl.pallas_call(slab_kernel, out_shape=jax.ShapeDtypeStruct(x.shape, x.dty...  19.3 us
    pallas_call x1, Pallas kernels, update_volume(): pl.pallas_call(update_kernel, out_shape=jax.ShapeDtypeStruct((CH, BOX, ZC...  14.4 us
    unnamed x22, local copies, waits for them, and re-layouts  3.97 us
    pallas_call x1, Pallas kernels, zpass(): pl.pallas_call(zpass_kernel, out_shape=jax.ShapeDtypeStruct((2, ZL * XL,...  3.05 us

profile of v1, /device:TPU:1, one launch (start us, length us, event | category | flops | bytes accessed | tf_op | source)
XLA Modules:
  0.0 103.3 jit_solution(832756347760073635)
XLA Ops:
  0.0 0.9 fusion
  1.0 0.0 copy-start
  1.0 1.7 %copy-done = bf16[32,48,768]{2,1,0:T(8,128)(2,1)S(1)} copy-done((bf16[32,48,768]{2,1,0:T(8,128)(2,1)S(1)}, bf16[32,48,768]{2,1,0:T(8,128)(2,1)}, u32[]{:S(2)}) %copy-start) | copy-done | bytes 2359320
  2.6 0.0 copy-start.4
  2.6 1.0 copy-done.4
  3.6 0.0 copy-start.7
  3.6 0.7 copy-done.7
  4.2 0.0 copy-start.8
  4.2 0.7 copy-done.8
  4.9 0.0 copy-start.6
  4.9 1.4 %local_sums.1 = (f32[8,48,768]{2,1,0:T(8,128)S(1)}, f32[8,128]{1,0:T(8,128)S(1)}) custom-call(s32[32]{0:T(128)S(1)} %copy-done.7, s32[32]{0:T(128)S(1)} %copy-done.8, bf16[32,48,768]{2,1,0:T(8,128)(2,1)S(1)} %copy-done, bf16[8,48,384]{2,1,0:T(8,128)(2,1)S(1)} %copy-done.4), custom_call_target="tpu_custom_call" | custom-call | tf_op jit(solution)/shard_map/local_sums/pallas_call | solution.py:68
  6.3 0.0 copy-start.1
  6.3 0.0 copy-start.5
  6.3 0.0 copy-start.9
  6.4 0.0 copy-start.10
  6.4 30.6 %reduce_sums.1 = (f32[384,768]{1,0:T(8,128)S(1)}, f32[8,128]{1,0:T(8,128)S(1)}, bf16[2,48,768]{2,1,0:T(8,128)(2,1)S(1)}) custom-call(f32[384,768]{1,0:T(8,128)S(1)} %bitcast.4, f32[8,128]{1,0:T(8,128)S(1)} %get-tuple-element.11.count_ref, bf16[2,48,768]{2,1,0:T(8,128)(2,1)S(1)} %pad_maximum_fusion.edge_ref), custom_call_target="tpu_custom_call" | custom-call | tf_op jit(solution)/shard_map/reduce_sums/pallas_call | solution.py:210
  37.0 0.0 copy-done.6
  37.0 0.0 copy-done.1
  37.0 0.0 copy-done.5
  37.0 0.0 copy-done.9
  37.0 0.0 copy-done.10
  37.0 14.4 %update_volume.1 = bf16[3,384,384]{2,1,0:T(8,128)(2,1)S(1)} custom-call(f32[384,768]{1,0:T(8,128)S(1)} %get-tuple-element.12.sum_ref, f32[8,128]{1,0:T(8,128)S(1)} %get-tuple-element.13.count_ref, bf16[2,48,768]{2,1,0:T(8,128)(2,1)S(1)} %get-tuple-element.14.halo_ref, bf16[12,48,768]{2,1,0:T(8,128)(2,1)S(1)} %copy-done.1, bf16[8,48,384]{2,1,0:T(8,128)(2,1)S(1)} %copy-done.5, ...), custom_call_target="tpu_custom_call" | custom-call | tf_op jit(solution)/shard_map/update_volume/pallas_call | solution.py:308
  51.5 0.0 copy-start.3
  51.5 28.2 %batch_exchange.1.in_ref = bf16[3,8,48,384]{3,2,1,0:T(8,128)(2,1)S(1)} custom-call(bf16[3,8,48,384]{3,2,1,0:T(8,128)(2,1)S(1)} %bitcast.3), custom_call_target="tpu_custom_call" | custom-call | tf_op jit(solution)/shard_map/batch_exchange/pallas_call | solution.py:356
  79.7 0.0 copy-done.3
  79.7 1.2 %ypass.1.in_ref = bf16[32,24,640]{2,1,0:T(8,128)(2,1)S(1)} custom-call(bf16[3,8,48,384]{3,2,1,0:T(8,128)(2,1)S(1)} %batch_exchange.1.in_ref, bf16[768,768]{1,0:T(8,128)(2,1)S(1)} %copy-done.3), custom_call_target="tpu_custom_call" | custom-call | tf_op jit(solution)/shard_map/ypass/pallas_call | solution.py:379
  80.9 0.0 copy-start.2
  80.9 19.3 %slab_exchange.1.in_ref = bf16[32,24,640]{2,1,0:T(8,128)(2,1)S(1)} custom-call(bf16[32,24,640]{2,1,0:T(8,128)(2,1)S(1)} %ypass.1.in_ref), custom_call_target="tpu_custom_call" | custom-call | tf_op jit(solution)/shard_map/slab_exchange/pallas_call | solution.py:426
  100.2 0.0 copy-done.2
  100.2 3.1 %zpass.1 = f32[2,576,384]{2,1,0:T(8,128)} custom-call(bf16[32,24,640]{2,1,0:T(8,128)(2,1)S(1)} %slab_exchange.1.in_ref, bf16[768,768]{1,0:T(8,128)(2,1)S(1)} %copy-done.2), custom_call_target="tpu_custom_call" | custom-call | tf_op jit(solution)/shard_map/zpass/pallas_call | solution.py:461
  (1 shorter events, 0.0 us)
Async XLA Ops:
  1.0 1.7 %copy-start = (bf16[32,48,768]{2,1,0:T(8,128)(2,1)S(1)}, bf16[32,48,768]{2,1,0:T(8,128)(2,1)}, u32[]{:S(2)}) copy-start(bf16[32,48,768]{2,1,0:T(8,128)(2,1)} %image_ref.1) | copy-start | bytes 7077892
  2.6 1.0 copy-start.4
  3.6 0.7 copy-start.7
  4.2 0.7 copy-start.8
  4.9 32.1 %copy-start.6 = (bf16[384,768]{1,0:T(8,128)(2,1)S(1)}, bf16[384,768]{1,0:T(8,128)(2,1)}, u32[]{:S(2)}) copy-start(bf16[384,768]{1,0:T(8,128)(2,1)} %constant.10.xtab_ref) | copy-start | bytes 1769476
  6.3 30.7 %copy-start.1 = (bf16[12,48,768]{2,1,0:T(8,128)(2,1)S(1)}, bf16[12,48,768]{2,1,0:T(8,128)(2,1)}, u32[]{:S(2)}) copy-start(bf16[12,48,768]{2,1,0:T(8,128)(2,1)} %vol_ref.1) | copy-start | bytes 2654212
  6.3 30.7 %copy-start.5 = (bf16[8,48,384]{2,1,0:T(8,128)(2,1)S(1)}, bf16[8,48,384]{2,1,0:T(8,128)(2,1)}, u32[]{:S(2)}) copy-start(bf16[8,48,384]{2,1,0:T(8,128)(2,1)} %ctf_ref.3) | copy-start | bytes 884740
  6.3 30.7 %copy-start.9 = (s32[8]{0:T(128)S(1)}, s32[8]{0:T(128)}, u32[]{:S(2)}) copy-start(s32[8]{0:T(128)} %tz_ref.1) | copy-start | bytes 100
  6.4 30.7 %copy-start.10 = (s32[8]{0:T(128)S(1)}, s32[8]{0:T(128)}, u32[]{:S(2)}) copy-start(s32[8]{0:T(128)} %tx_ref.1) | copy-start | bytes 100
  51.5 28.2 %copy-start.3 = (bf16[768,768]{1,0:T(8,128)(2,1)S(1)}, bf16[768,768]{1,0:T(8,128)(2,1)}, u32[]{:S(2)}) copy-start(bf16[768,768]{1,0:T(8,128)(2,1)} %constant.11.ytab_ref) | copy-start | bytes 3538948
  80.9 19.3 %copy-start.2 = (bf16[768,768]{1,0:T(8,128)(2,1)S(1)}, bf16[768,768]{1,0:T(8,128)(2,1)}, u32[]{:S(2)}) copy-start(bf16[768,768]{1,0:T(8,128)(2,1)} %constant.12.ztab_ref) | copy-start | bytes 3538948

commit v2 on v0

v2 whole, which is shorter than its diff:
```python
import functools
import math

import jax
import jax.numpy as jnp
import numpy as np
from jax import lax
from jax.experimental import pallas as pl
from jax.experimental.pallas import tpu as pltpu
from jax.sharding import PartitionSpec as P

TAU = 1.0
BOX = 384
HALF = 192
ORI = 8
DEF = 8
NS = 32
NB = 8
ZL = BOX // NS
YL = BOX // NB
XL = BOX // NB
CH = 3
ZC = ZL // CH
PIECE = 24
CHIPS = NS // 2
LANES = 640
F32 = jnp.float32
BF16 = jnp.bfloat16
VMEM = pl.BlockSpec(memory_space=pltpu.VMEM)
SMEM = pl.BlockSpec(memory_space=pltpu.SMEM)
LIMIT = 58 * 1024 * 1024


def dft_tables():
    index = np.arange(BOX, dtype=np.int64)
    phases = (index[:, None] * index[None, :] % BOX).astype(np.float64)
    angles = phases * (2.0 * math.pi / BOX)
    factor = 1.0 / math.sqrt(BOX)
    return np.cos(angles) * factor, np.sin(angles) * factor


def pass_tables():
    cos, sin = dft_tables()
    x_tab = np.concatenate([cos, -sin], axis=0).T
    full = np.stack([np.stack([cos, sin], 1), np.stack([-sin, cos], 1)], 0)
    y_tab = full.reshape(2, NB, YL, 2, NS, ZL).transpose(4, 3, 5, 1, 0, 2).reshape(2 * BOX, 2 * BOX)
    z_tab = full.reshape(2, NS, ZL, 2, BOX).transpose(2, 0, 1, 3, 4).reshape(2 * BOX, 2 * BOX)
    return tuple(jnp.asarray(t.astype(np.float32), F32).astype(BF16) for t in (x_tab, y_tab, z_tab))


def sums_kernel(orient_ref, defocus_ref, image_ref, ctf_ref, sum_ref, count_ref):
    block = pl.program_id(0)
    count = image_ref.shape[0]
    row = lax.broadcasted_iota(jnp.int32, count_ref.shape, 0)
    lane = lax.broadcasted_iota(jnp.int32, count_ref.shape, 1)

    @pl.when(block == 0)
    def _():
        sum_ref[...] = jnp.zeros_like(sum_ref)
        count_ref[...] = jnp.zeros_like(count_ref)

    def step(i, total):
        p = block * count + i
        orient, defocus = orient_ref[p], defocus_ref[p]
        ctf = ctf_ref[defocus].astype(F32)
        for h in range(2):
            cols = slice(h * BOX, (h + 1) * BOX)
            sum_ref[orient, :, cols] += ctf * image_ref[i, :, cols].astype(F32)
        return total + jnp.where((row == orient) & (lane == defocus), 1.0, 0.0)

    count_ref[...] = lax.fori_loop(0, count, step, count_ref[...])


def local_sums(orient_ids, defocus_ids, images, ctf_tables):
    block = 8
    whole = lambda *shape: pl.BlockSpec(shape, lambda i: (0,) * len(shape))
    return pl.pallas_call(
        sums_kernel,
        grid=(images.shape[0] // block,),
        out_shape=(
            jax.ShapeDtypeStruct((ORI, YL, 2 * BOX), F32),
            jax.ShapeDtypeStruct((8, 128), F32),
        ),
        in_specs=[
            SMEM,
            SMEM,
            pl.BlockSpec((block, YL, 2 * BOX), lambda i: (i, 0, 0)),
            whole(DEF, YL, BOX),
        ],
        out_specs=(whole(ORI, YL, 2 * BOX), whole(8, 128)),
        compiler_params=pltpu.CompilerParams(vmem_limit_bytes=LIMIT),
        name="local_sums",
    )(orient_ids, defocus_ids, images, ctf_tables)


def slab_copy(src, dst, send, recv, to):
    return pltpu.make_async_remote_copy(
        src_ref=src, dst_ref=dst, send_sem=send, recv_sem=recv,
        device_id={"slab": to}, device_id_type=pl.DeviceIdType.MESH,
    )


def batch_copy(src, dst, send, recv, to):
    return pltpu.make_async_remote_copy(
        src_ref=src, dst_ref=dst, send_sem=send, recv_sem=recv,
        device_id={"batch": to}, device_id_type=pl.DeviceIdType.MESH,
    )


def interp_row(tilt):
    column = lax.broadcasted_iota(jnp.int32, (1, BOX), 1)
    position = HALF * 256 + (column - HALF) * tilt
    low = position >> 8
    fraction = (position & 255).astype(F32) * (1.0 / 256.0)
    return low, fraction


OFFSETS = [(2, 2), (3, 2), (2, 3), (1, 2), (2, 1), (0, 2), (2, 0), (3, 1), (1, 3), (3, 3), (1, 1), (0, 3), (0, 1), (3, 0), (1, 0)]
GROUPS = ((0, 2), (2, 3))


def main_kernel(
    sum_ref, count_ref, volume_ref, ctf_ref, tz_ref, tx_ref, xtab_ref, ytab_ref,
    out_ref,
    vol, ctf_buf, x_tab, y_tab, width, depth, proj, numer, power, operand, weight, paired,
    pair_buf, piece_buf, part_buf, total_buf, sums, count_buf, count_pair,
    along_x, pieces, gathered, along_y,
    load, pair_send, pair_recv, part_send, part_recv, gather_send, gather_recv, twin_send, twin_recv,
    count_send, count_recv, halo_send, halo_recv, batch_send, batch_recv, batch_own, slab_send, slab_recv, slab_own,
):
    me = lax.axis_index("slab")
    row_block = lax.axis_index("batch")
    core = lax.rem(me, 2)
    chip = me // 2
    chip_x = lax.rem(chip, 4)
    chip_y = chip // 4
    twin = me + 1 - 2 * core
    below = lax.rem(me + NS - 1, NS)
    above = lax.rem(me + 1, NS)

    loads = [
        pltpu.make_async_copy(volume_ref, vol.at[pl.ds(1, ZL)], load.at[0]),
        pltpu.make_async_copy(ctf_ref, ctf_buf, load.at[1]),
        pltpu.make_async_copy(xtab_ref, x_tab, load.at[2]),
        pltpu.make_async_copy(ytab_ref, y_tab, load.at[3]),
    ]
    for copy in loads:
        copy.start()

    def chip_at(d):
        x, y = OFFSETS[d]
        return 4 * lax.rem(chip_y + y, 4) + lax.rem(chip_x + x, 4)

    def chip_from(d):
        x, y = OFFSETS[d]
        return 4 * lax.rem(chip_y + 4 - y, 4) + lax.rem(chip_x + 4 - x, 4)

    mesh_id = pl.DeviceIdType.MESH
    barrier = pltpu.get_barrier_semaphore()

    def greet(d, _):
        pl.semaphore_signal(barrier, inc=1, device_id={"slab": lax.rem(me + d, NS)}, device_id_type=mesh_id)
        return 0

    lax.fori_loop(1, NS, greet, 0)

    def greet_batch(d, _):
        pl.semaphore_signal(barrier, inc=1, device_id={"batch": lax.rem(row_block + d, NB)}, device_id_type=mesh_id)
        return 0

    lax.fori_loop(1, NB, greet_batch, 0)

    plane = lax.broadcasted_iota(jnp.int32, (16, BOX), 0) + (me * ZL - 1)
    column = lax.broadcasted_iota(jnp.int32, (BOX, BOX), 0)
    for o in range(ORI):
        low, frac = interp_row(tz_ref[o])
        weights = jnp.where(plane == low, 1.0 - frac, 0.0) + jnp.where(plane == low + 1, frac, 0.0)
        depth[o] = jnp.where(plane < BOX, weights, 0.0)
        low, frac = interp_row(tx_ref[o])
        table = jnp.where(column == low, 1.0 - frac, 0.0) + jnp.where(column == low + 1, frac, 0.0)
        width[:, o * BOX : (o + 1) * BOX] = table.astype(BF16)

    pl.semaphore_wait(barrier, NS + NB - 2)

    rows = ORI * YL // 2
    keep = pl.multiple_of(rows * core, rows)
    give = pl.multiple_of(rows * (1 - core), rows)
    pair = slab_copy(sum_ref.at[pl.ds(give, rows)], pair_buf, pair_send, pair_recv, twin)
    pair.start()
    count_twin = slab_copy(count_ref, count_pair, count_send.at[15], count_recv.at[15], twin)
    count_twin.start()
    loads[0].wait()
    halo_up = slab_copy(vol.at[ZL], vol.at[0], halo_send.at[0], halo_recv.at[0], above)
    halo_up.start()
    halo_down = slab_copy(vol.at[1], vol.at[ZL + 1], halo_send.at[1], halo_recv.at[1], below)
    halo_down.start()

    def project(o):
        for h in range(2):
            cols = slice(h * BOX, (h + 1) * BOX)
            seen = jnp.dot(
                vol[:, :, cols].reshape((ZL + 2) * YL, BOX), width[:, o * BOX : (o + 1) * BOX],
                preferred_element_type=F32,
            ).reshape(ZL + 2, YL, BOX)
            total = jnp.zeros((YL, BOX), F32)
            for j in range(ZL + 2):
                total = total + depth[o, j : j + 1, :] * seen[j]
            proj[o, :, cols] = total

    count_twin.wait()
    count_buf[15] = count_ref[...] + count_pair[...]
    counts = [
        slab_copy(count_buf.at[15], count_buf.at[d], count_send.at[d], count_recv.at[d], 2 * chip_at(d) + core)
        for d in range(15)
    ]
    for copy in counts:
        copy.start()
    halo_up.wait()
    halo_down.wait()
    project(0)
    project(1)

    pair.wait()
    for j in range(CHIPS):
        r, c = PIECE * (j // 2), BOX * (j % 2)
        piece_buf[j] = (
            sum_ref[pl.ds(pl.multiple_of(keep + r, 8), PIECE), c : c + BOX] + pair_buf[r : r + PIECE, c : c + BOX]
        )
    parts = [
        slab_copy(piece_buf.at[chip_at(d)], part_buf.at[d], part_send.at[d], part_recv.at[d], 2 * chip_at(d) + core)
        for d in range(15)
    ]
    for copy in parts:
        copy.start()
    for o in range(2, ORI):
        project(o)
    total = piece_buf[chip]
    for d in range(15):
        parts[d].wait()
        total = total + part_buf[d]
    total_buf[...] = total

    def place(ref, which):
        r = pl.multiple_of(keep + PIECE * (which // 2), 8)
        c = pl.multiple_of(BOX * lax.rem(which, 2), 128)
        return ref.at[pl.ds(r, PIECE), pl.ds(c, BOX)]

    gathers = [
        slab_copy(total_buf, place(sums, chip), gather_send.at[d], gather_recv.at[d], 2 * chip_at(d) + core)
        for d in range(15)
    ]
    for copy in gathers:
        copy.start()
    own_r = pl.multiple_of(keep + PIECE * (chip // 2), 8)
    own_c = pl.multiple_of(BOX * lax.rem(chip, 2), 128)
    sums[pl.ds(own_r, PIECE), pl.ds(own_c, BOX)] = total_buf[...]
    twins = [
        slab_copy(place(sums, w), place(sums, w), twin_send.at[d], twin_recv.at[d], twin)
        for d, w in enumerate([chip_from(d) for d in range(15)] + [chip])
    ]
    twins[15].start()

    number = count_buf[15]
    for d in range(15):
        counts[d].wait()
        number = number + count_buf[d]
    loads[1].wait()
    ctf = ctf_buf[...].astype(F32)
    square = ctf * ctf
    for o in range(ORI):
        have = jnp.zeros((YL, BOX), F32)
        for d in range(DEF):
            have = have + number[o : o + 1, d : d + 1] * square[d]
        power[o] = have
        k = slice(o * BOX, (o + 1) * BOX)
        for z in range(ZL):
            operand[z * YL : (z + 1) * YL, k] = (depth[o, z + 1 : z + 2, :] * have).astype(BF16)
    weight[...] = lax.dot_general(
        operand[...], width[...], (((1,), (1,)), ((), ())), preferred_element_type=F32
    ) + TAU

    for d in range(15):
        gathers[d].wait()
        twins[d].start()
    for d in range(16):
        twins[d].wait()
    for o in range(ORI):
        for h in range(2):
            cols = slice(h * BOX, (h + 1) * BOX)
            numer[o, :, cols] = sums[o * YL : (o + 1) * YL, cols] - power[o] * proj[o, :, cols]

    loads[2].wait()

    def batch_piece(c, d):
        to = lax.rem(row_block + d, NB)
        return batch_copy(along_x.at[c, to], pieces.at[c, row_block], batch_send.at[c, d], batch_recv.at[c, d], to)

    def batch_local(c):
        return pltpu.make_async_copy(along_x.at[c, row_block], pieces.at[c, row_block], batch_own.at[c])

    for c in range(CH):
        for o in range(ORI):
            k = slice(o * BOX, (o + 1) * BOX)
            for zi in range(ZC):
                w = depth[o, c * ZC + zi + 1 : c * ZC + zi + 2, :]
                for h in range(2):
                    r = (zi * 2 + h) * YL
                    operand[r : r + YL, k] = (w * numer[o, :, h * BOX : (h + 1) * BOX]).astype(BF16)
        back = lax.dot_general(
            operand[: 2 * ZC * YL, :], width[...], (((1,), (1,)), ((), ())), preferred_element_type=F32
        )
        for zi in range(ZC):
            z = c * ZC + zi
            part = []
            for h in range(2):
                r = (zi * 2 + h) * YL
                old = vol[z + 1, :, h * BOX : (h + 1) * BOX].astype(F32)
                part.append((old + back[r : r + YL] / weight[z * YL : (z + 1) * YL, :]).astype(BF16))
            r = zi * 2 * YL
            paired[r : r + YL, :BOX] = part[0]
            paired[r : r + YL, BOX:] = part[1]
            paired[r + YL : r + 2 * YL, :BOX] = part[1]
            paired[r + YL : r + 2 * YL, BOX:] = -part[0]
        along_x[c] = lax.dot_general(
            x_tab[...], paired[...], (((1,), (1,)), ((), ())), preferred_element_type=F32
        ).astype(BF16).reshape(NB, XL, ZC * 2 * YL)
        for d in (4, 3, 5, 2, 6, 1, 7):
            batch_piece(c, d).start()
        batch_local(c).start()

    loads[3].wait()

    def slab_piece(g, d, e):
        lanes = pl.ds(GROUPS[g][0] * ZC * XL, (384, 256)[g])
        to = 2 * chip_at(d) + (core if e == 0 else 1 - core) if d < 15 else twin
        return slab_copy(
            along_y.at[to, :, lanes], out_ref.at[me, :, lanes], slab_send.at[g, 2 * d + e], slab_recv.at[g, 2 * d + e], to
        )

    def slab_local(g):
        lanes = pl.ds(GROUPS[g][0] * ZC * XL, (384, 256)[g])
        return pltpu.make_async_copy(along_y.at[me, :, lanes], out_ref.at[me, :, lanes], slab_own.at[g])

    targets = [(d, e) for d in range(15) for e in range(2)] + [(15, 0)]
    along_y[:, :, ZL * XL :] = jnp.zeros((NS, 2 * ZL, LANES - ZL * XL), BF16)
    for g, (first, last) in enumerate(GROUPS):
        for c in range(first, last):
            for d in range(1, NB):
                batch_piece(c, d).wait()
            batch_local(c).wait()
            for zi in range(ZC):
                z = c * ZC + zi
                lanes = slice(zi * 2 * YL, (zi + 1) * 2 * YL)
                gathered[z * XL : (z + 1) * XL, :] = jnp.concatenate(
                    [pieces[c, b, :, lanes] for b in range(NB)], axis=1
                )
        low, high = first * ZC * XL, last * ZC * XL
        out = lax.dot_general(
            y_tab[...], gathered[low:high, :], (((1,), (1,)), ((), ())), preferred_element_type=F32
        )
        along_y[:, :, low:high] = out.astype(BF16).reshape(NS, 2 * ZL, high - low)
        for d, e in targets:
            slab_piece(g, d, e).start()
        slab_local(g).start()
    for g in range(len(GROUPS)):
        for d, e in targets:
            slab_piece(g, d, e).wait()
        slab_local(g).wait()


def main(sums, counts, volume, ctf_tables, tilt_z, tilt_x, x_tab, y_tab):
    dma = pltpu.SemaphoreType.DMA
    any_space = pl.BlockSpec(memory_space=pl.ANY)
    half = ORI * YL // 2
    return pl.pallas_call(
        main_kernel,
        out_shape=jax.ShapeDtypeStruct((NS, 2 * ZL, LANES), BF16),
        in_specs=[VMEM, VMEM, any_space, any_space, SMEM, SMEM, any_space, any_space],
        out_specs=VMEM,
        scratch_shapes=[
            pltpu.VMEM((ZL + 2, YL, 2 * BOX), BF16),
            pltpu.VMEM((DEF, YL, BOX), BF16),
            pltpu.VMEM((BOX, 2 * BOX), BF16),
            pltpu.VMEM((2 * BOX, 2 * BOX), BF16),
            pltpu.VMEM((BOX, ORI * BOX), BF16),
            pltpu.VMEM((ORI, 16, BOX), F32),
            pltpu.VMEM((ORI, YL, 2 * BOX), F32),
            pltpu.VMEM((ORI, YL, 2 * BOX), F32),
            pltpu.VMEM((ORI, YL, BOX), F32),
            pltpu.VMEM((ZL * YL, ORI * BOX), BF16),
            pltpu.VMEM((ZL * YL, BOX), F32),
            pltpu.VMEM((ZC * 2 * YL, 2 * BOX), BF16),
            pltpu.VMEM((half, 2 * BOX), F32),
            pltpu.VMEM((CHIPS, PIECE, BOX), F32),
            pltpu.VMEM((CHIPS - 1, PIECE, BOX), F32),
            pltpu.VMEM((PIECE, BOX), F32),
            pltpu.VMEM((ORI * YL, 2 * BOX), F32),
            pltpu.VMEM((CHIPS, 8, 128), F32),
            pltpu.VMEM((8, 128), F32),
            pltpu.VMEM((CH, NB, XL, ZC * 2 * YL), BF16),
            pltpu.VMEM((CH, NB, XL, ZC * 2 * YL), BF16),
            pltpu.VMEM((ZL * XL, 2 * BOX), BF16),
            pltpu.VMEM((NS, 2 * ZL, LANES), BF16),
            dma((4,)), dma(()), dma(()), dma((15,)), dma((15,)), dma((15,)), dma((15,)), dma((16,)), dma((16,)),
            dma((16,)), dma((16,)), dma((2,)), dma((2,)), dma((CH, NB)), dma((CH, NB)), dma((CH,)),
            dma((2, 32)), dma((2, 32)), dma((2,)),
        ],
        compiler_params=pltpu.CompilerParams(vmem_limit_bytes=LIMIT, collective_id=0, has_side_effects=True),
        name="main",
    )(sums, counts, volume, ctf_tables, tilt_z, tilt_x, x_tab, y_tab)


def zpass_kernel(in_ref, ztab_ref, out_ref, wide, gathered):
    for t in range(LANES // 128):
        lanes = slice(t * 128, (t + 1) * 128)
        wide[t] = in_ref[:, :, lanes].astype(F32).reshape(NS * 2 * ZL, 128)
    for z in range(ZL):
        lane = z * XL
        t, off = lane // 128, lane % 128
        for h in range(2):
            blocks = []
            for y in range(ZL):
                rows = pl.ds(h * ZL + y, NS, 2 * ZL)
                if off + XL <= 128:
                    blocks.append(wide[t, rows, :][:, off : off + XL])
                else:
                    both = jnp.concatenate([wide[t, rows, :], wide[t + 1, rows, :]], axis=1)
                    blocks.append(both[:, off : off + XL])
            r = (z * 2 + h) * NS
            gathered[r : r + NS, :] = jnp.concatenate(blocks, axis=1).astype(BF16)
    out = lax.dot_general(gathered[...], ztab_ref[...], (((0,), (0,)), ((), ())), preferred_element_type=F32)
    out_ref[0] = out[:, :BOX]
    out_ref[1] = out[:, BOX:]


def zpass(x, z_tab):
    return pl.pallas_call(
        zpass_kernel,
        out_shape=jax.ShapeDtypeStruct((2, ZL * XL, BOX), F32),
        in_specs=[VMEM, VMEM],
        out_specs=VMEM,
        scratch_shapes=[
            pltpu.VMEM((LANES // 128, NS * 2 * ZL, 128), F32),
            pltpu.VMEM((2 * BOX, ZL * XL), BF16),
        ],
        compiler_params=pltpu.CompilerParams(vmem_limit_bytes=LIMIT),
        name="zpass",
    )(x, z_tab)


def local(volume, images, orient_ids, defocus_ids, ctf_tables, tilt_z, tilt_x):
    x_tab, y_tab, z_tab = pass_tables()
    sums, counts = local_sums(orient_ids, defocus_ids, images, ctf_tables)
    pieces = main(
        sums.reshape(ORI * YL, 2 * BOX), counts, volume, ctf_tables, tilt_z, tilt_x, x_tab, y_tab
    )
    return zpass(pieces, z_tab).reshape(2, ZL, XL, BOX)


def solution(mesh):
    in_specs = (
        P("slab", "batch", None),
        P("slab", "batch", None),
        P("slab"),
        P("slab"),
        P(None, "batch", None),
        P(),
        P(),
    )
    out_specs = P(None, "slab", "batch", None)
    return jax.shard_map(local, mesh=mesh, in_specs=in_specs, out_specs=out_specs, check_vma=False)
```

time: 452 us -> 80.6 us (0.18); the launches traced: 444 us -> 80.5 us
  waiting for transfers between devices: 228 us -> 0 us
  Pallas kernels: 0 us -> 80.4 us
  local copies, waits for them, and re-layouts: 73.3 us -> 0 us
  matrix products: 68.1 us -> 0 us
  blocking collectives: 53.6 us -> 0 us
  between operations: 14.4 us -> 0.01 us
  other arithmetic: 6.39 us -> 0 us
    psum x2 -> x0, waiting for transfers between devices: 228 us -> none  [the longest x1 116 us: local(): numer_sums, ctf_power = lax.psum((numer_local, ctf_power), 'slab')]
    pallas_call x0 -> x3, Pallas kernels: none -> 80.4 us  [the longest x1 71.8 us: main(): pl.pallas_call(main_kernel, out_shape=jax.ShapeDtypeStruct((NS, 2 * ZL, L...]
    dot_general x36 -> x0, matrix products: 58.2 us -> none  [the longest x8 13.4 us: local(): jnp.einsum('zycx,xk->zyck', volume_cube, width_tab[orient], preferred_ele...]
    all_to_all x2 -> x0, blocking collectives: 53.6 us -> none  [the longest x1 30.7 us: local(): lax.all_to_all(along_x, 'batch', split_axis=3, concat_axis=1, tiled=True)]
    unnamed x62 -> x0, local copies, waits for them, and re-layouts: 33.6 us -> none
    another operation x11 -> x0, local copies, waits for them, and re-layouts: 15.5 us -> none  [the longest x9 11.1 us: local(): partials = jnp.stack(partial_list)]
    slice x4 -> x0, local copies, waits for them, and re-layouts: 11.1 us -> none  [the longest x1 5.94 us: local(): numer_sums[orient][None]]
    unnamed x4 -> x0, matrix products: 9.89 us -> none
  transfers between devices with their start and end apart: 2 -> 0, of which waited for: 2 -> 0; matrix products, arithmetic and copies ran while one was open for 2% -> 0% of each run, Pallas kernels for 0% -> 0%
where the time goes in v2:
time: 80.6 us; the launch traced here: 80.5 us
  Pallas kernels  80.4 us (100%)
    pallas_call x1, Pallas kernels, main(): pl.pallas_call(main_kernel, out_shape=jax.ShapeDtypeStruct((NS, 2 * ZL, L...  71.8 us
    pallas_call x1, Pallas kernels, zpass(): pl.pallas_call(zpass_kernel, out_shape=jax.ShapeDtypeStruct((2, ZL * XL,...  4.63 us
    pallas_call x1, Pallas kernels, local_sums(): pl.pallas_call(sums_kernel, grid=(images.shape[0] // block,), out_shape=(...  3.99 us

profile of v2, /device:TPU:1, one launch (start us, length us, event | category | flops | bytes accessed | tf_op | source)
XLA Modules:
  0.0 80.5 jit_solution(13261546460816842807)
XLA Ops:
  0.0 4.0 %local_sums.1 = (f32[8,48,768]{2,1,0:T(8,128)}, f32[8,128]{1,0:T(8,128)}) custom-call(s32[32]{0:T(128)} %orient_ref.1, s32[32]{0:T(128)} %defocus_ref.1, bf16[32,48,768]{2,1,0:T(8,128)(2,1)} %image_ref.1, bf16[8,48,384]{2,1,0:T(8,128)(2,1)} %ctf_ref.3), custom_call_target="tpu_custom_call" | custom-call | tf_op jit(solution)/shard_map/local_sums/pallas_call | solution.py:77
  4.0 71.8 %main.1.in_ref = bf16[32,24,640]{2,1,0:T(8,128)(2,1)} custom-call(f32[384,768]{1,0:T(8,128)} %bitcast.2, f32[8,128]{1,0:T(8,128)} %get-tuple-element.8.count_ref, bf16[12,48,768]{2,1,0:T(8,128)(2,1)} %volume_ref.1, bf16[8,48,384]{2,1,0:T(8,128)(2,1)} %ctf_ref.3, s32[8]{0:T(128)} %tz_ref.1, s32[8]{0:T(128)} %tx_ref.1, bf16[384,768]{1,0:T(8,128)(2,1)} %constant.10.xtab_ref, ...), custom_call_target="tpu_custom_call" | custom-call | tf_op jit(solution)/shard_map/main/pallas_call | solution.py:375
  75.8 4.6 %zpass.1 = f32[2,576,384]{2,1,0:T(8,128)} custom-call(bf16[32,24,640]{2,1,0:T(8,128)(2,1)} %main.1.in_ref, bf16[768,768]{1,0:T(8,128)(2,1)} %constant.12.ztab_ref), custom_call_target="tpu_custom_call" | custom-call | tf_op jit(solution)/shard_map/zpass/pallas_call | solution.py:437

commit v3 on v2

v3 whole, which is shorter than its diff:
```python
import functools
import math

import jax
import jax.numpy as jnp
import numpy as np
from jax import lax
from jax.experimental import pallas as pl
from jax.experimental.pallas import tpu as pltpu
from jax.sharding import PartitionSpec as P

TAU = 1.0
BOX = 384
HALF = 192
ORI = 8
DEF = 8
NS = 32
NB = 8
ZL = BOX // NS
YL = BOX // NB
XL = BOX // NB
CH = 3
ZC = ZL // CH
PARTS = ((0, 16), (16, 32))
CHIPS = NS // 2
LANES = 640
F32 = jnp.float32
BF16 = jnp.bfloat16
VMEM = pl.BlockSpec(memory_space=pltpu.VMEM)
SMEM = pl.BlockSpec(memory_space=pltpu.SMEM)
LIMIT = 58 * 1024 * 1024


def dft_tables():
    index = np.arange(BOX, dtype=np.int64)
    phases = (index[:, None] * index[None, :] % BOX).astype(np.float64)
    angles = phases * (2.0 * math.pi / BOX)
    factor = 1.0 / math.sqrt(BOX)
    return np.cos(angles) * factor, np.sin(angles) * factor


def pass_tables():
    cos, sin = dft_tables()
    x_tab = np.concatenate([cos, -sin], axis=0).T
    full = np.stack([np.stack([cos, sin], 1), np.stack([-sin, cos], 1)], 0)
    split = full.reshape(2, NB, YL, 2, NS, ZL).transpose(4, 3, 5, 1, 0, 2)
    y_tab = np.concatenate(
        [split[..., y : y + n].reshape(2 * BOX, NB * 2 * n) for y, n in PARTS], axis=1
    )
    z_tab = full.reshape(2, NS, ZL, 2, BOX).transpose(2, 0, 1, 3, 4).reshape(2 * BOX, 2 * BOX)
    return tuple(jnp.asarray(t.astype(np.float32), F32).astype(BF16) for t in (x_tab, y_tab, z_tab))


def slab_copy(src, dst, send, recv, to):
    return pltpu.make_async_remote_copy(
        src_ref=src, dst_ref=dst, send_sem=send, recv_sem=recv,
        device_id={"slab": to}, device_id_type=pl.DeviceIdType.MESH,
    )


def batch_copy(src, dst, send, recv, to):
    return pltpu.make_async_remote_copy(
        src_ref=src, dst_ref=dst, send_sem=send, recv_sem=recv,
        device_id={"batch": to}, device_id_type=pl.DeviceIdType.MESH,
    )


def interp_row(tilt):
    column = lax.broadcasted_iota(jnp.int32, (1, BOX), 1)
    position = HALF * 256 + (column - HALF) * tilt
    low = position >> 8
    fraction = (position & 255).astype(F32) * (1.0 / 256.0)
    return low, fraction


OFFSETS = [(2, 2), (3, 2), (2, 3), (1, 2), (2, 1), (0, 2), (2, 0), (3, 1), (1, 3), (3, 3), (1, 1), (0, 3), (0, 1), (3, 0), (1, 0)]
GROUPS = ((0, 2), (2, 3))


def main_kernel(
    orient_ref, defocus_ref, tz_ref, tx_ref, image_ref, volume_ref, ctf_ref, xtab_ref, ytab_ref,
    out_ref,
    image0, image1, vol, ctf_buf, x_tab, y_tab, width, depth, proj, power, operand, weight, paired,
    local0, local1, pair0, pair1, piece0, piece1, part0, part1, total0, total1, sums0, sums1,
    count_buf, count_pair, count_own,
    along0, along1, pieces0, pieces1, gathered, along_y,
    load, pair_send, pair_recv, part_send, part_recv, gather_send, gather_recv, twin_send, twin_recv,
    count_send, count_recv, halo_send, halo_recv, batch_send, batch_recv, batch_own, slab_send, slab_recv, slab_own,
):
    me = lax.axis_index("slab")
    row_block = lax.axis_index("batch")
    core = lax.rem(me, 2)
    chip = me // 2
    chip_x = lax.rem(chip, 4)
    chip_y = chip // 4
    twin = me + 1 - 2 * core
    below = lax.rem(me + NS - 1, NS)
    above = lax.rem(me + 1, NS)
    images, locals_, pairs = (image0, image1), (local0, local1), (pair0, pair1)
    pieces_, parts_, totals, sums = (piece0, piece1), (part0, part1), (total0, total1), (sums0, sums1)

    loads = [
        pltpu.make_async_copy(src, dst, load.at[i])
        for i, (src, dst) in enumerate([
            (ctf_ref, ctf_buf),
            (image_ref.at[:, pl.ds(PARTS[0][0], PARTS[0][1])], image0),
            (image_ref.at[:, pl.ds(PARTS[1][0], PARTS[1][1])], image1),
            (volume_ref, vol.at[pl.ds(1, ZL)]),
            (xtab_ref, x_tab),
            (ytab_ref, y_tab),
        ])
    ]
    for copy in loads:
        copy.start()

    def chip_at(d):
        x, y = OFFSETS[d]
        return 4 * lax.rem(chip_y + y, 4) + lax.rem(chip_x + x, 4)

    def chip_from(d):
        x, y = OFFSETS[d]
        return 4 * lax.rem(chip_y + 4 - y, 4) + lax.rem(chip_x + 4 - x, 4)

    mesh_id = pl.DeviceIdType.MESH
    barrier = pltpu.get_barrier_semaphore()

    def greet(d, _):
        pl.semaphore_signal(barrier, inc=1, device_id={"slab": lax.rem(me + d, NS)}, device_id_type=mesh_id)
        return 0

    lax.fori_loop(1, NS, greet, 0)

    def greet_batch(d, _):
        pl.semaphore_signal(barrier, inc=1, device_id={"batch": lax.rem(row_block + d, NB)}, device_id_type=mesh_id)
        return 0

    lax.fori_loop(1, NB, greet_batch, 0)

    plane = lax.broadcasted_iota(jnp.int32, (16, BOX), 0) + (me * ZL - 1)
    column = lax.broadcasted_iota(jnp.int32, (BOX, BOX), 0)
    for o in range(ORI):
        low, frac = interp_row(tz_ref[o])
        weights = jnp.where(plane == low, 1.0 - frac, 0.0) + jnp.where(plane == low + 1, frac, 0.0)
        depth[o] = jnp.where(plane < BOX, weights, 0.0)
        low, frac = interp_row(tx_ref[o])
        table = jnp.where(column == low, 1.0 - frac, 0.0) + jnp.where(column == low + 1, frac, 0.0)
        width[:, o * BOX : (o + 1) * BOX] = table.astype(BF16)

    def local_sums(part):
        for r in range(0, PARTS[part][1], 16):
            for t in range(0, BOX, 128):
                def step(p, totals_):
                    orient, defocus = orient_ref[p], defocus_ref[p]
                    ctf = ctf_buf[defocus, PARTS[part][0] + r : PARTS[part][0] + r + 16, t : t + 128].astype(F32)
                    terms = [
                        ctf * images[part][p, r : r + 16, h * BOX + t : h * BOX + t + 128].astype(F32) for h in range(2)
                    ]
                    hot = [jnp.where(orient == o, 1.0, 0.0) for o in range(ORI)]
                    return tuple(totals_[2 * o + h] + hot[o] * terms[h] for o in range(ORI) for h in range(2))

                have = lax.fori_loop(0, 32, step, tuple(jnp.zeros((16, 128), F32) for _ in range(2 * ORI)))
                for o in range(ORI):
                    for h in range(2):
                        row = o * PARTS[part][1] + r
                        locals_[part][row : row + 16, h * BOX + t : h * BOX + t + 128] = have[2 * o + h]

    loads[0].wait()
    loads[1].wait()
    local_sums(0)

    pl.semaphore_wait(barrier, NS + NB - 2)

    def half(part):
        rows = ORI * PARTS[part][1] // 2
        return rows, pl.multiple_of(rows * core, rows), pl.multiple_of(rows * (1 - core), rows)

    def pair_copy(part):
        rows, _, give = half(part)
        return slab_copy(
            locals_[part].at[pl.ds(give, rows)], pairs[part], pair_send.at[part], pair_recv.at[part], twin
        )

    pair_copy(0).start()
    row = lax.broadcasted_iota(jnp.int32, (8, 128), 0)
    lane = lax.broadcasted_iota(jnp.int32, (8, 128), 1)

    def count_step(p, have):
        return have + jnp.where((row == orient_ref[p]) & (lane == defocus_ref[p]), 1.0, 0.0)

    count_own[...] = lax.fori_loop(0, 32, count_step, jnp.zeros((8, 128), F32))
    count_twin = slab_copy(count_own, count_pair, count_send.at[15], count_recv.at[15], twin)
    count_twin.start()
    loads[3].wait()
    halo_up = slab_copy(vol.at[ZL], vol.at[0], halo_send.at[0], halo_recv.at[0], above)
    halo_up.start()
    halo_down = slab_copy(vol.at[1], vol.at[ZL + 1], halo_send.at[1], halo_recv.at[1], below)
    halo_down.start()
    loads[2].wait()
    local_sums(1)
    pair_copy(1).start()

    def part_copies(part):
        return [
            slab_copy(
                pieces_[part].at[chip_at(d)], parts_[part].at[d],
                part_send.at[part, d], part_recv.at[part, d], 2 * chip_at(d) + core,
            )
            for d in range(15)
        ]

    def spread_pieces(part):
        _, keep, _ = half(part)
        n = PARTS[part][1] // 2
        pair_copy(part).wait()
        for j in range(CHIPS):
            r, c = n * (j // 2), BOX * (j % 2)
            pieces_[part][j] = (
                locals_[part][pl.ds(pl.multiple_of(keep + r, 8), n), c : c + BOX]
                + pairs[part][r : r + n, c : c + BOX]
            )
        for copy in part_copies(part):
            copy.start()

    def place(part, which):
        _, keep, _ = half(part)
        n = PARTS[part][1] // 2
        r = pl.multiple_of(keep + n * (which // 2), 8)
        c = pl.multiple_of(BOX * lax.rem(which, 2), 128)
        return pl.ds(r, n), pl.ds(c, BOX)

    def gather_copies(part):
        return [
            slab_copy(
                totals[part], sums[part].at[place(part, chip)],
                gather_send.at[part, d], gather_recv.at[part, d], 2 * chip_at(d) + core,
            )
            for d in range(15)
        ]

    def twin_copies(part):
        return [
            slab_copy(
                sums[part].at[place(part, w)], sums[part].at[place(part, w)],
                twin_send.at[part, d], twin_recv.at[part, d], twin,
            )
            for d, w in enumerate([chip_from(d) for d in range(15)] + [chip])
        ]

    def add_pieces(part):
        total = pieces_[part][chip]
        for d, copy in enumerate(part_copies(part)):
            copy.wait()
            total = total + parts_[part][d]
        totals[part][...] = total
        for copy in gather_copies(part):
            copy.start()
        sums[part][place(part, chip)] = total
        twin_copies(part)[15].start()

    def forward_pieces(part):
        for gather, forward in zip(gather_copies(part), twin_copies(part)[:15]):
            gather.wait()
            forward.start()

    def take_sums(part):
        for copy in twin_copies(part):
            copy.wait()

    def project(part, o):
        y, n = PARTS[part]
        for h in range(2):
            cols = slice(h * BOX, (h + 1) * BOX)
            seen = jnp.dot(
                vol[:, y : y + n, cols].reshape((ZL + 2) * n, BOX), width[:, o * BOX : (o + 1) * BOX],
                preferred_element_type=F32,
            ).reshape(ZL + 2, n, BOX)
            total = jnp.zeros((n, BOX), F32)
            for j in range(ZL + 2):
                total = total + depth[o, j : j + 1, :] * seen[j]
            proj[o, y : y + n, cols] = total

    spread_pieces(0)
    count_twin.wait()
    count_buf[15] = count_own[...] + count_pair[...]
    counts = [
        slab_copy(count_buf.at[15], count_buf.at[d], count_send.at[d], count_recv.at[d], 2 * chip_at(d) + core)
        for d in range(15)
    ]
    for copy in counts:
        copy.start()
    halo_up.wait()
    halo_down.wait()
    for o in range(4):
        project(0, o)
    spread_pieces(1)
    for o in range(4, ORI):
        project(0, o)
    add_pieces(0)

    number = count_buf[15]
    for d in range(15):
        counts[d].wait()
        number = number + count_buf[d]
    ctf_all = ctf_buf[...].astype(F32)
    square = ctf_all * ctf_all
    for o in range(ORI):
        have = jnp.zeros((YL, BOX), F32)
        for d in range(DEF):
            have = have + number[o : o + 1, d : d + 1] * square[d]
        power[o] = have
        k = slice(o * BOX, (o + 1) * BOX)
        for z in range(ZL):
            operand[z * YL : (z + 1) * YL, k] = (depth[o, z + 1 : z + 2, :] * have).astype(BF16)
    weight[...] = lax.dot_general(
        operand[...], width[...], (((1,), (1,)), ((), ())), preferred_element_type=F32
    ) + TAU
    add_pieces(1)
    forward_pieces(0)
    for o in range(2):
        project(1, o)
    take_sums(0)
    loads[4].wait()

    def update(part, first, last):
        y, n = PARTS[part]
        count = last - first
        for o in range(ORI):
            k = slice(o * BOX, (o + 1) * BOX)
            for h in range(2):
                cols = slice(h * BOX, (h + 1) * BOX)
                numer = sums[part][o * n : (o + 1) * n, cols] - power[o, y : y + n, :] * proj[o, y : y + n, cols]
                for zi in range(count):
                    r = (zi * 2 + h) * n
                    w = depth[o, first + zi + 1 : first + zi + 2, :]
                    operand[r : r + n, k] = (w * numer).astype(BF16)
        m = count * 2 * n
        back = lax.dot_general(
            operand[:m, :], width[...], (((1,), (1,)), ((), ())), preferred_element_type=F32
        )
        for zi in range(count):
            z = first + zi
            fresh = []
            for h in range(2):
                r = (zi * 2 + h) * n
                old = vol[z + 1, y : y + n, h * BOX : (h + 1) * BOX].astype(F32)
                fresh.append((old + back[r : r + n] / weight[z * YL + y : z * YL + y + n, :]).astype(BF16))
            r = zi * 2 * n
            paired[r : r + n, :BOX] = fresh[0]
            paired[r : r + n, BOX:] = fresh[1]
            paired[r + n : r + 2 * n, :BOX] = fresh[1]
            paired[r + n : r + 2 * n, BOX:] = -fresh[0]
        return lax.dot_general(
            x_tab[...], paired[:m, :], (((1,), (1,)), ((), ())), preferred_element_type=F32
        ).astype(BF16).reshape(NB, XL, m)

    def batch_piece(c, d):
        to = lax.rem(row_block + d, NB)
        src = along0.at[to] if c == 0 else along1.at[c - 1, to]
        dst = pieces0.at[row_block] if c == 0 else pieces1.at[c - 1, row_block]
        return batch_copy(src, dst, batch_send.at[c, d], batch_recv.at[c, d], to)

    def batch_local(c):
        src = along0.at[row_block] if c == 0 else along1.at[c - 1, row_block]
        dst = pieces0.at[row_block] if c == 0 else pieces1.at[c - 1, row_block]
        return pltpu.make_async_copy(src, dst, batch_own.at[c])

    def batch_go(c):
        for d in (4, 3, 5, 2, 6, 1, 7):
            batch_piece(c, d).start()
        batch_local(c).start()

    def batch_done(c):
        for d in range(1, NB):
            batch_piece(c, d).wait()
        batch_local(c).wait()

    along0[...] = update(0, 0, ZL)
    batch_go(0)
    forward_pieces(1)
    for o in range(2, ORI):
        project(1, o)
    take_sums(1)
    for c in range(CH):
        along1[c] = update(1, c * ZC, (c + 1) * ZC)
        batch_go(c + 1)

    loads[5].wait()

    def slab_piece(g, d, e):
        lanes = pl.ds(GROUPS[g][0] * ZC * XL, (384, 256)[g])
        to = 2 * chip_at(d) + (core if e == 0 else 1 - core) if d < 15 else twin
        return slab_copy(
            along_y.at[to, :, lanes], out_ref.at[me, :, lanes], slab_send.at[g, 2 * d + e], slab_recv.at[g, 2 * d + e], to
        )

    def slab_local(g):
        lanes = pl.ds(GROUPS[g][0] * ZC * XL, (384, 256)[g])
        return pltpu.make_async_copy(along_y.at[me, :, lanes], out_ref.at[me, :, lanes], slab_own.at[g])

    targets = [(d, e) for d in range(15) for e in range(2)] + [(15, 0)]
    along_y[:, :, ZL * XL :] = jnp.zeros((NS, 2 * ZL, LANES - ZL * XL), BF16)
    wide0, wide1 = (2 * n for _, n in PARTS)
    batch_done(0)
    for z in range(ZL):
        gathered[z * XL : (z + 1) * XL, : NB * wide0] = jnp.concatenate(
            [pieces0[b, :, z * wide0 : (z + 1) * wide0] for b in range(NB)], axis=1
        )
    for g, (first, last) in enumerate(GROUPS):
        for c in range(first, last):
            batch_done(c + 1)
            for zi in range(ZC):
                z = c * ZC + zi
                gathered[z * XL : (z + 1) * XL, NB * wide0 :] = jnp.concatenate(
                    [pieces1[c, b, :, zi * wide1 : (zi + 1) * wide1] for b in range(NB)], axis=1
                )
        low, high = first * ZC * XL, last * ZC * XL
        out = lax.dot_general(
            y_tab[...], gathered[low:high, :], (((1,), (1,)), ((), ())), preferred_element_type=F32
        )
        along_y[:, :, low:high] = out.astype(BF16).reshape(NS, 2 * ZL, high - low)
        for d, e in targets:
            slab_piece(g, d, e).start()
        slab_local(g).start()
    for g in range(len(GROUPS)):
        for d, e in targets:
            slab_piece(g, d, e).wait()
        slab_local(g).wait()


def main(orient_ids, defocus_ids, tilt_z, tilt_x, images, volume, ctf_tables, x_tab, y_tab):
    dma = pltpu.SemaphoreType.DMA
    any_space = pl.BlockSpec(memory_space=pl.ANY)
    two = lambda shape, dtype: [pltpu.VMEM(shape(n), dtype) for _, n in PARTS]
    return pl.pallas_call(
        main_kernel,
        out_shape=jax.ShapeDtypeStruct((NS, 2 * ZL, LANES), BF16),
        in_specs=[SMEM] * 4 + [any_space] * 5,
        out_specs=VMEM,
        scratch_shapes=[
            *two(lambda n: (32, n, 2 * BOX), BF16),
            pltpu.VMEM((ZL + 2, YL, 2 * BOX), BF16),
            pltpu.VMEM((DEF, YL, BOX), BF16),
            pltpu.VMEM((BOX, 2 * BOX), BF16),
            pltpu.VMEM((2 * BOX, 2 * BOX), BF16),
            pltpu.VMEM((BOX, ORI * BOX), BF16),
            pltpu.VMEM((ORI, 16, BOX), F32),
            pltpu.VMEM((ORI, YL, 2 * BOX), F32),
            pltpu.VMEM((ORI, YL, BOX), F32),
            pltpu.VMEM((ZL * YL, ORI * BOX), BF16),
            pltpu.VMEM((ZL * YL, BOX), F32),
            pltpu.VMEM((BOX, 2 * BOX), BF16),
            *two(lambda n: (ORI * n, 2 * BOX), F32),
            *two(lambda n: (ORI * n // 2, 2 * BOX), F32),
            *two(lambda n: (CHIPS, n // 2, BOX), F32),
            *two(lambda n: (CHIPS - 1, n // 2, BOX), F32),
            *two(lambda n: (n // 2, BOX), F32),
            *two(lambda n: (ORI * n, 2 * BOX), F32),
            pltpu.VMEM((CHIPS, 8, 128), F32),
            pltpu.VMEM((8, 128), F32),
            pltpu.VMEM((8, 128), F32),
            pltpu.VMEM((NB, XL, ZL * 2 * PARTS[0][1]), BF16),
            pltpu.VMEM((CH, NB, XL, ZC * 2 * PARTS[1][1]), BF16),
            pltpu.VMEM((NB, XL, ZL * 2 * PARTS[0][1]), BF16),
            pltpu.VMEM((CH, NB, XL, ZC * 2 * PARTS[1][1]), BF16),
            pltpu.VMEM((ZL * XL, 2 * BOX), BF16),
            pltpu.VMEM((NS, 2 * ZL, LANES), BF16),
            dma((6,)), dma((2,)), dma((2,)), dma((2, 15)), dma((2, 15)), dma((2, 15)), dma((2, 15)),
            dma((2, 16)), dma((2, 16)), dma((16,)), dma((16,)), dma((2,)), dma((2,)),
            dma((CH + 1, NB)), dma((CH + 1, NB)), dma((CH + 1,)), dma((2, 32)), dma((2, 32)), dma((2,)),
        ],
        compiler_params=pltpu.CompilerParams(vmem_limit_bytes=LIMIT, collective_id=0, has_side_effects=True),
        name="main",
    )(orient_ids, defocus_ids, tilt_z, tilt_x, images, volume, ctf_tables, x_tab, y_tab)


def zpass_kernel(in_ref, ztab_ref, out_ref, wide, gathered):
    for t in range(LANES // 128):
        lanes = slice(t * 128, (t + 1) * 128)
        wide[t] = in_ref[:, :, lanes].astype(F32).reshape(NS * 2 * ZL, 128)
    for z in range(ZL):
        lane = z * XL
        t, off = lane // 128, lane % 128
        for h in range(2):
            blocks = []
            for y in range(ZL):
                rows = pl.ds(h * ZL + y, NS, 2 * ZL)
                if off + XL <= 128:
                    blocks.append(wide[t, rows, :][:, off : off + XL])
                else:
                    both = jnp.concatenate([wide[t, rows, :], wide[t + 1, rows, :]], axis=1)
                    blocks.append(both[:, off : off + XL])
            r = (z * 2 + h) * NS
            gathered[r : r + NS, :] = jnp.concatenate(blocks, axis=1).astype(BF16)
    out = lax.dot_general(gathered[...], ztab_ref[...], (((0,), (0,)), ((), ())), preferred_element_type=F32)
    out_ref[0] = out[:, :BOX]
    out_ref[1] = out[:, BOX:]


def zpass(x, z_tab):
    return pl.pallas_call(
        zpass_kernel,
        out_shape=jax.ShapeDtypeStruct((2, ZL * XL, BOX), F32),
        in_specs=[VMEM, VMEM],
        out_specs=VMEM,
        scratch_shapes=[
            pltpu.VMEM((LANES // 128, NS * 2 * ZL, 128), F32),
            pltpu.VMEM((2 * BOX, ZL * XL), BF16),
        ],
        compiler_params=pltpu.CompilerParams(vmem_limit_bytes=LIMIT),
        name="zpass",
    )(x, z_tab)


def local(volume, images, orient_ids, defocus_ids, ctf_tables, tilt_z, tilt_x):
    x_tab, y_tab, z_tab = pass_tables()
    pieces = main(orient_ids, defocus_ids, tilt_z, tilt_x, images, volume, ctf_tables, x_tab, y_tab)
    return zpass(pieces, z_tab).reshape(2, ZL, XL, BOX)


def solution(mesh):
    in_specs = (
        P("slab", "batch", None),
        P("slab", "batch", None),
        P("slab"),
        P("slab"),
        P(None, "batch", None),
        P(),
        P(),
    )
    out_specs = P(None, "slab", "batch", None)
    return jax.shard_map(local, mesh=mesh, in_specs=in_specs, out_specs=out_specs, check_vma=False)
```

time: 80.6 us -> 73.5 us (0.912)
  Pallas kernels: 80.4 us -> 73.4 us
    pallas_call x1 -> x0, Pallas kernels: 3.99 us -> none  [local_sums(): pl.pallas_call(sums_kernel, grid=(images.shape[0] // block,), out_shape=(...]
    pallas_call x1, Pallas kernels: 71.8 us -> 68.8 us  [main(): pl.pallas_call(main_kernel, out_shape=jax.ShapeDtypeStruct((NS, 2 * ZL, L...]
where the time goes in v3:
time: 73.5 us; the launch traced here: 73.4 us
  Pallas kernels  73.4 us (100%)
    pallas_call x1, Pallas kernels, main(): pl.pallas_call(main_kernel, out_shape=jax.ShapeDtypeStruct((NS, 2 * ZL, L...  68.8 us
    pallas_call x1, Pallas kernels, zpass(): pl.pallas_call(zpass_kernel, out_shape=jax.ShapeDtypeStruct((2, ZL * XL,...  4.64 us

profile of v3, /device:TPU:1, one launch (start us, length us, event | category | flops | bytes accessed | tf_op | source)
XLA Modules:
  0.0 73.4 jit_solution(17617837555024428452)
XLA Ops:
  0.0 68.8 %main.1.in_ref = bf16[32,24,640]{2,1,0:T(8,128)(2,1)} custom-call(s32[32]{0:T(128)} %orient_ref.1, s32[32]{0:T(128)} %defocus_ref.1, s32[8]{0:T(128)} %tz_ref.1, s32[8]{0:T(128)} %tx_ref.1, bf16[32,48,768]{2,1,0:T(8,128)(2,1)} %image_ref.1, bf16[12,48,768]{2,1,0:T(8,128)(2,1)} %volume_ref.1, bf16[8,48,384]{2,1,0:T(8,128)(2,1)} %ctf_ref.1, ...), custom_call_target="tpu_custom_call" | custom-call | tf_op jit(solution)/shard_map/main/pallas_call | solution.py:434
  68.8 4.6 %zpass.1 = f32[2,576,384]{2,1,0:T(8,128)} custom-call(bf16[32,24,640]{2,1,0:T(8,128)(2,1)} %main.1.in_ref, bf16[768,768]{1,0:T(8,128)(2,1)} %constant.12.ztab_ref), custom_call_target="tpu_custom_call" | custom-call | tf_op jit(solution)/shard_map/zpass/pallas_call | solution.py:500

commit v4 on v3

--- a/solution.py
+++ b/solution.py
@@ -83,9 +83,9 @@
     image0, image1, vol, ctf_buf, x_tab, y_tab, width, depth, proj, power, operand, weight, paired,
     local0, local1, pair0, pair1, piece0, piece1, part0, part1, total0, total1, sums0, sums1,
     count_buf, count_pair, count_own,
-    along0, along1, pieces0, pieces1, gathered, along_y,
+    along0, along1, pieces0, pieces1, gathered, along_y, landed, wide, turned,
     load, pair_send, pair_recv, part_send, part_recv, gather_send, gather_recv, twin_send, twin_recv,
-    count_send, count_recv, halo_send, halo_recv, batch_send, batch_recv, batch_own, slab_send, slab_recv, slab_own,
+    count_send, count_recv, halo_send, halo_recv, batch_send, batch_recv, batch_own, slab_send, slab_recv, slab_own, store,
 ):
     me = lax.axis_index("slab")
     row_block = lax.axis_index("batch")
@@ -98,6 +98,29 @@
     above = lax.rem(me + 1, NS)
     images, locals_, pairs = (image0, image1), (local0, local1), (pair0, pair1)
     pieces_, parts_, totals, sums = (piece0, piece1), (part0, part1), (total0, total1), (sums0, sums1)
+
+    def chip_at(d):
+        x, y = OFFSETS[d]
+        return 4 * lax.rem(chip_y + y, 4) + lax.rem(chip_x + x, 4)
+
+    def chip_from(d):
+        x, y = OFFSETS[d]
+        return 4 * lax.rem(chip_y + 4 - y, 4) + lax.rem(chip_x + 4 - x, 4)
+
+    mesh_id = pl.DeviceIdType.MESH
+    barrier = pltpu.get_barrier_semaphore()
+
+    def greet(d, _):
+        pl.semaphore_signal(barrier, inc=1, device_id={"slab": lax.rem(me + d, NS)}, device_id_type=mesh_id)
+        return 0
+
+    lax.fori_loop(1, NS, greet, 0)
+
+    def greet_batch(d, _):
+        pl.semaphore_signal(barrier, inc=1, device_id={"batch": lax.rem(row_block + d, NB)}, device_id_type=mesh_id)
+        return 0
+
+    lax.fori_loop(1, NB, greet_batch, 0)
 
     loads = [
         pltpu.make_async_copy(src, dst, load.at[i])
@@ -113,39 +136,6 @@
     for copy in loads:
         copy.start()
 
-    def chip_at(d):
-        x, y = OFFSETS[d]
-        return 4 * lax.rem(chip_y + y, 4) + lax.rem(chip_x + x, 4)
-
-    def chip_from(d):
-        x, y = OFFSETS[d]
-        return 4 * lax.rem(chip_y + 4 - y, 4) + lax.rem(chip_x + 4 - x, 4)
-
-    mesh_id = pl.DeviceIdType.MESH
-    barrier = pltpu.get_barrier_semaphore()
-
-    def greet(d, _):
-        pl.semaphore_signal(barrier, inc=1, device_id={"slab": lax.rem(me + d, NS)}, device_id_type=mesh_id)
-        return 0
-
-    lax.fori_loop(1, NS, greet, 0)
-
-    def greet_batch(d, _):
-        pl.semaphore_signal(barrier, inc=1, device_id={"batch": lax.rem(row_block + d, NB)}, device_id_type=mesh_id)
-        return 0
-
-    lax.fori_loop(1, NB, greet_batch, 0)
-
-    plane = lax.broadcasted_iota(jnp.int32, (16, BOX), 0) + (me * ZL - 1)
-    column = lax.broadcasted_iota(jnp.int32, (BOX, BOX), 0)
-    for o in range(ORI):
-        low, frac = interp_row(tz_ref[o])
-        weights = jnp.where(plane == low, 1.0 - frac, 0.0) + jnp.where(plane == low + 1, frac, 0.0)
-        depth[o] = jnp.where(plane < BOX, weights, 0.0)
-        low, frac = interp_row(tx_ref[o])
-        table = jnp.where(column == low, 1.0 - frac, 0.0) + jnp.where(column == low + 1, frac, 0.0)
-        width[:, o * BOX : (o + 1) * BOX] = table.astype(BF16)
-
     def local_sums(part):
         for r in range(0, PARTS[part][1], 16):
             for t in range(0, BOX, 128):
@@ -158,7 +148,7 @@
                     hot = [jnp.where(orient == o, 1.0, 0.0) for o in range(ORI)]
                     return tuple(totals_[2 * o + h] + hot[o] * terms[h] for o in range(ORI) for h in range(2))
 
-                have = lax.fori_loop(0, 32, step, tuple(jnp.zeros((16, 128), F32) for _ in range(2 * ORI)))
+                have = lax.fori_loop(0, 32, step, tuple(jnp.zeros((16, 128), F32) for _ in range(2 * ORI)), unroll=4)
                 for o in range(ORI):
                     for h in range(2):
                         row = o * PARTS[part][1] + r
@@ -167,6 +157,14 @@
     loads[0].wait()
     loads[1].wait()
     local_sums(0)
+    row = lax.broadcasted_iota(jnp.int32, (8, 128), 0)
+    lane = lax.broadcasted_iota(jnp.int32, (8, 128), 1)
+
+    def count_step(p, have):
+        return have + jnp.where((row == orient_ref[p]) & (lane == defocus_ref[p]), 1.0, 0.0)
+
+    count_own[...] = lax.fori_loop(0, 32, count_step, jnp.zeros((8, 128), F32), unroll=4)
+    loads[3].wait()
 
     pl.semaphore_wait(barrier, NS + NB - 2)
 
@@ -181,16 +179,8 @@
         )
 
     pair_copy(0).start()
-    row = lax.broadcasted_iota(jnp.int32, (8, 128), 0)
-    lane = lax.broadcasted_iota(jnp.int32, (8, 128), 1)
-
-    def count_step(p, have):
-        return have + jnp.where((row == orient_ref[p]) & (lane == defocus_ref[p]), 1.0, 0.0)
-
-    count_own[...] = lax.fori_loop(0, 32, count_step, jnp.zeros((8, 128), F32))
     count_twin = slab_copy(count_own, count_pair, count_send.at[15], count_recv.at[15], twin)
     count_twin.start()
-    loads[3].wait()
     halo_up = slab_copy(vol.at[ZL], vol.at[0], halo_send.at[0], halo_recv.at[0], above)
     halo_up.start()
     halo_down = slab_copy(vol.at[1], vol.at[ZL + 1], halo_send.at[1], halo_recv.at[1], below)
@@ -237,14 +227,18 @@
             for d in range(15)
         ]
 
-    def twin_copies(part):
+    def twin_copies(part, own=False):
         return [
             slab_copy(
                 sums[part].at[place(part, w)], sums[part].at[place(part, w)],
                 twin_send.at[part, d], twin_recv.at[part, d], twin,
             )
-            for d, w in enumerate([chip_from(d) for d in range(15)] + [chip])
+            for d, w in enumerate([chip_from(d) for d in range(15)] + ([chip] if own else []))
         ]
+
+    def twin_own(part):
+        spot = sums[part].at[place(part, chip)]
+        return slab_copy(spot, spot, twin_send.at[part, 15], twin_recv.at[part, 15], twin)
 
     def add_pieces(part):
         total = pieces_[part][chip]
@@ -255,15 +249,15 @@
         for copy in gather_copies(part):
             copy.start()
         sums[part][place(part, chip)] = total
-        twin_copies(part)[15].start()
+        twin_own(part).start()
 
     def forward_pieces(part):
-        for gather, forward in zip(gather_copies(part), twin_copies(part)[:15]):
+        for gather, forward in list(zip(gather_copies(part), twin_copies(part)))[::-1]:
             gather.wait()
             forward.start()
 
     def take_sums(part):
-        for copy in twin_copies(part):
+        for copy in twin_copies(part, True):
             copy.wait()
 
     def project(part, o):
@@ -280,6 +274,16 @@
             proj[o, y : y + n, cols] = total
 
     spread_pieces(0)
+    plane = lax.broadcasted_iota(jnp.int32, (16, BOX), 0) + (me * ZL - 1)
+    column = lax.broadcasted_iota(jnp.int32, (BOX, BOX), 0)
+    for o in range(ORI):
+        low, frac = interp_row(tz_ref[o])
+        weights = jnp.where(plane == low, 1.0 - frac, 0.0) + jnp.where(plane == low + 1, frac, 0.0)
+        depth[o] = jnp.where(plane < BOX, weights, 0.0)
+        low, frac = interp_row(tx_ref[o])
+        table = jnp.where(column == low, 1.0 - frac, 0.0) + jnp.where(column == low + 1, frac, 0.0)
+        width[:, o * BOX : (o + 1) * BOX] = table.astype(BF16)
+
     count_twin.wait()
     count_buf[15] = count_own[...] + count_pair[...]
     counts = [
@@ -290,33 +294,38 @@
         copy.start()
     halo_up.wait()
     halo_down.wait()
-    for o in range(4):
-        project(0, o)
     spread_pieces(1)
-    for o in range(4, ORI):
+    for o in range(ORI):
         project(0, o)
     add_pieces(0)
+
+    def weigh(part):
+        y, n = PARTS[part]
+        ctf = ctf_buf[:, y : y + n, :].astype(F32)
+        square = ctf * ctf
+        for o in range(ORI):
+            have = jnp.zeros((n, BOX), F32)
+            for d in range(DEF):
+                have = have + number[o : o + 1, d : d + 1] * square[d]
+            power[o, y : y + n, :] = have
+            k = slice(o * BOX, (o + 1) * BOX)
+            for z in range(ZL):
+                operand[z * n : (z + 1) * n, k] = (depth[o, z + 1 : z + 2, :] * have).astype(BF16)
+        back = lax.dot_general(
+            operand[: ZL * n, :], width[...], (((1,), (1,)), ((), ())), preferred_element_type=F32
+        )
+        weight[:, y : y + n, :] = back.reshape(ZL, n, BOX) + TAU
 
     number = count_buf[15]
     for d in range(15):
         counts[d].wait()
         number = number + count_buf[d]
-    ctf_all = ctf_buf[...].astype(F32)
-    square = ctf_all * ctf_all
-    for o in range(ORI):
-        have = jnp.zeros((YL, BOX), F32)
-        for d in range(DEF):
-            have = have + number[o : o + 1, d : d + 1] * square[d]
-        power[o] = have
-        k = slice(o * BOX, (o + 1) * BOX)
-        for z in range(ZL):
-            operand[z * YL : (z + 1) * YL, k] = (depth[o, z + 1 : z + 2, :] * have).astype(BF16)
-    weight[...] = lax.dot_general(
-        operand[...], width[...], (((1,), (1,)), ((), ())), preferred_element_type=F32
-    ) + TAU
+    weigh(0)
     add_pieces(1)
+    for o in range(3):
+        project(1, o)
     forward_pieces(0)
-    for o in range(2):
+    for o in range(3, 5):
         project(1, o)
     take_sums(0)
     loads[4].wait()
@@ -343,7 +352,7 @@
             for h in range(2):
                 r = (zi * 2 + h) * n
                 old = vol[z + 1, y : y + n, h * BOX : (h + 1) * BOX].astype(F32)
-                fresh.append((old + back[r : r + n] / weight[z * YL + y : z * YL + y + n, :]).astype(BF16))
+                fresh.append((old + back[r : r + n] / weight[z, y : y + n, :]).astype(BF16))
             r = zi * 2 * n
             paired[r : r + n, :BOX] = fresh[0]
             paired[r : r + n, BOX:] = fresh[1]
@@ -376,9 +385,10 @@
 
     along0[...] = update(0, 0, ZL)
     batch_go(0)
+    for o in range(5, ORI):
+        project(1, o)
+    weigh(1)
     forward_pieces(1)
-    for o in range(2, ORI):
-        project(1, o)
     take_sums(1)
     for c in range(CH):
         along1[c] = update(1, c * ZC, (c + 1) * ZC)
@@ -390,12 +400,12 @@
         lanes = pl.ds(GROUPS[g][0] * ZC * XL, (384, 256)[g])
         to = 2 * chip_at(d) + (core if e == 0 else 1 - core) if d < 15 else twin
         return slab_copy(
-            along_y.at[to, :, lanes], out_ref.at[me, :, lanes], slab_send.at[g, 2 * d + e], slab_recv.at[g, 2 * d + e], to
+            along_y.at[to, :, lanes], landed.at[me, :, lanes], slab_send.at[g, 2 * d + e], slab_recv.at[g, 2 * d + e], to
         )
 
     def slab_local(g):
         lanes = pl.ds(GROUPS[g][0] * ZC * XL, (384, 256)[g])
-        return pltpu.make_async_copy(along_y.at[me, :, lanes], out_ref.at[me, :, lanes], slab_own.at[g])
+        return pltpu.make_async_copy(along_y.at[me, :, lanes], landed.at[me, :, lanes], slab_own.at[g])
 
     targets = [(d, e) for d in range(15) for e in range(2)] + [(15, 0)]
     along_y[:, :, ZL * XL :] = jnp.zeros((NS, 2 * ZL, LANES - ZL * XL), BF16)
@@ -421,10 +431,31 @@
         for d, e in targets:
             slab_piece(g, d, e).start()
         slab_local(g).start()
+    stores = []
     for g in range(len(GROUPS)):
         for d, e in targets:
             slab_piece(g, d, e).wait()
         slab_local(g).wait()
+        for t in ((0, 1, 2), (3, 4))[g]:
+            wide[t] = landed[:, :, t * 128 : (t + 1) * 128].astype(F32).reshape(NS * 2 * ZL, 128)
+        for z in range(GROUPS[g][0] * ZC, GROUPS[g][1] * ZC):
+            t, off = z * XL // 128, z * XL % 128
+            for h in range(2):
+                blocks = []
+                for y in range(ZL):
+                    spot = pl.ds(h * ZL + y, NS, 2 * ZL)
+                    if off + XL <= 128:
+                        blocks.append(wide[t, spot, :][:, off : off + XL])
+                    else:
+                        both = jnp.concatenate([wide[t, spot, :], wide[t + 1, spot, :]], axis=1)
+                        blocks.append(both[:, off : off + XL])
+                r = (z * 2 + h) * NS
+                turned[r : r + NS, :] = jnp.concatenate(blocks, axis=1).astype(BF16)
+        done = pl.ds(GROUPS[g][0] * ZC * 2 * NS, (GROUPS[g][1] - GROUPS[g][0]) * ZC * 2 * NS)
+        stores.append(pltpu.make_async_copy(turned.at[done], out_ref.at[done], store.at[g]))
+        stores[g].start()
+    for copy in stores:
+        copy.wait()
 
 
 def main(orient_ids, defocus_ids, tilt_z, tilt_x, images, volume, ctf_tables, x_tab, y_tab):
@@ -433,9 +464,9 @@
     two = lambda shape, dtype: [pltpu.VMEM(shape(n), dtype) for _, n in PARTS]
     return pl.pallas_call(
         main_kernel,
-        out_shape=jax.ShapeDtypeStruct((NS, 2 * ZL, LANES), BF16),
+        out_shape=jax.ShapeDtypeStruct((2 * BOX, ZL * XL), BF16),
         in_specs=[SMEM] * 4 + [any_space] * 5,
-        out_specs=VMEM,
+        out_specs=any_space,
         scratch_shapes=[
             *two(lambda n: (32, n, 2 * BOX), BF16),
             pltpu.VMEM((ZL + 2, YL, 2 * BOX), BF16),
@@ -447,7 +478,7 @@
             pltpu.VMEM((ORI, YL, 2 * BOX), F32),
             pltpu.VMEM((ORI, YL, BOX), F32),
             pltpu.VMEM((ZL * YL, ORI * BOX), BF16),
-            pltpu.VMEM((ZL * YL, BOX), F32),
+            pltpu.VMEM((ZL, YL, BOX), F32),
             pltpu.VMEM((BOX, 2 * BOX), BF16),
             *two(lambda n: (ORI * n, 2 * BOX), F32),
             *two(lambda n: (ORI * n // 2, 2 * BOX), F32),
@@ -464,47 +495,48 @@
             pltpu.VMEM((CH, NB, XL, ZC * 2 * PARTS[1][1]), BF16),
             pltpu.VMEM((ZL * XL, 2 * BOX), BF16),
             pltpu.VMEM((NS, 2 * ZL, LANES), BF16),
+            pltpu.VMEM((NS, 2 * ZL, LANES), BF16),
+            pltpu.VMEM((LANES // 128, NS * 2 * ZL, 128), F32),
+            pltpu.VMEM((2 * BOX, ZL * XL), BF16),
             dma((6,)), dma((2,)), dma((2,)), dma((2, 15)), dma((2, 15)), dma((2, 15)), dma((2, 15)),
             dma((2, 16)), dma((2, 16)), dma((16,)), dma((16,)), dma((2,)), dma((2,)),
-            dma((CH + 1, NB)), dma((CH + 1, NB)), dma((CH + 1,)), dma((2, 32)), dma((2, 32)), dma((2,)),
+            dma((CH + 1, NB)), dma((CH + 1, NB)), dma((CH + 1,)), dma((2, 32)), dma((2, 32)), dma((2,)), dma((2,)),
         ],
         compiler_params=pltpu.CompilerParams(vmem_limit_bytes=LIMIT, collective_id=0, has_side_effects=True),
         name="main",
     )(orient_ids, defocus_ids, tilt_z, tilt_x, images, volume, ctf_tables, x_tab, y_tab)
 
 
-def zpass_kernel(in_ref, ztab_ref, out_ref, wide, gathered):
-    for t in range(LANES // 128):
-        lanes = slice(t * 128, (t + 1) * 128)
-        wide[t] = in_ref[:, :, lanes].astype(F32).reshape(NS * 2 * ZL, 128)
-    for z in range(ZL):
-        lane = z * XL
-        t, off = lane // 128, lane % 128
-        for h in range(2):
-            blocks = []
-            for y in range(ZL):
-                rows = pl.ds(h * ZL + y, NS, 2 * ZL)
-                if off + XL <= 128:
-                    blocks.append(wide[t, rows, :][:, off : off + XL])
-                else:
-                    both = jnp.concatenate([wide[t, rows, :], wide[t + 1, rows, :]], axis=1)
-                    blocks.append(both[:, off : off + XL])
-            r = (z * 2 + h) * NS
-            gathered[r : r + NS, :] = jnp.concatenate(blocks, axis=1).astype(BF16)
-    out = lax.dot_general(gathered[...], ztab_ref[...], (((0,), (0,)), ((), ())), preferred_element_type=F32)
-    out_ref[0] = out[:, :BOX]
-    out_ref[1] = out[:, BOX:]
+def zpass_kernel(in_ref, ztab_ref, out_ref, x, tab, result, load, store):
+    loads = [pltpu.make_async_copy(in_ref, x, load.at[2])] + [
+        pltpu.make_async_copy(ztab_ref.at[:, pl.ds(h * BOX, BOX)], tab.at[h], load.at[h]) for h in range(2)
+    ]
+    for copy in loads:
+        copy.start()
+    loads[0].wait()
+    stores = []
+    for h in range(2):
+        loads[h + 1].wait()
+        result[h] = lax.dot_general(x[...], tab[h], (((0,), (0,)), ((), ())), preferred_element_type=F32)
+        stores.append(pltpu.make_async_copy(result.at[h], out_ref.at[h], store.at[h]))
+        stores[h].start()
+    for copy in stores:
+        copy.wait()
 
 
 def zpass(x, z_tab):
+    any_space = pl.BlockSpec(memory_space=pl.ANY)
     return pl.pallas_call(
         zpass_kernel,
         out_shape=jax.ShapeDtypeStruct((2, ZL * XL, BOX), F32),
-        in_specs=[VMEM, VMEM],
-        out_specs=VMEM,
+        in_specs=[any_space] * 2,
+        out_specs=any_space,
         scratch_shapes=[
-            pltpu.VMEM((LANES // 128, NS * 2 * ZL, 128), F32),
             pltpu.VMEM((2 * BOX, ZL * XL), BF16),
+            pltpu.VMEM((2, 2 * BOX, BOX), BF16),
+            pltpu.VMEM((2, ZL * XL, BOX), F32),
+            pltpu.SemaphoreType.DMA((3,)),
+            pltpu.SemaphoreType.DMA((2,)),
         ],
         compiler_params=pltpu.CompilerParams(vmem_limit_bytes=LIMIT),
         name="zpass",
@@ -513,8 +545,8 @@
 
 def local(volume, images, orient_ids, defocus_ids, ctf_tables, tilt_z, tilt_x):
     x_tab, y_tab, z_tab = pass_tables()
-    pieces = main(orient_ids, defocus_ids, tilt_z, tilt_x, images, volume, ctf_tables, x_tab, y_tab)
-    return zpass(pieces, z_tab).reshape(2, ZL, XL, BOX)
+    turned = main(orient_ids, defocus_ids, tilt_z, tilt_x, images, volume, ctf_tables, x_tab, y_tab)
+    return zpass(turned, z_tab).reshape(2, ZL, XL, BOX)
 
 
 def solution(mesh):

time: 73.5 us -> 70.2 us (0.955)
  Pallas kernels: 73.4 us -> 69.9 us
    pallas_call x1, Pallas kernels: 68.8 us -> 66.3 us  [main(): pl.pallas_call(main_kernel, out_shape=jax.ShapeDtypeStruct((2 * BOX, ZL *...]
    pallas_call x1, Pallas kernels: 4.64 us -> 3.62 us  [zpass(): pl.pallas_call(zpass_kernel, out_shape=jax.ShapeDtypeStruct((2, ZL * XL,...]
where the time goes in v4:
time: 70.2 us; the launch traced here: 70.1 us
  Pallas kernels  69.9 us (100%)
    pallas_call x1, Pallas kernels, main(): pl.pallas_call(main_kernel, out_shape=jax.ShapeDtypeStruct((2 * BOX, ZL *...  66.3 us
    pallas_call x1, Pallas kernels, zpass(): pl.pallas_call(zpass_kernel, out_shape=jax.ShapeDtypeStruct((2, ZL * XL,...  3.62 us

profile of v4, /device:TPU:1, one launch (start us, length us, event | category | flops | bytes accessed | tf_op | source)
XLA Modules:
  0.0 70.1 jit_solution(12587589434607680438)
XLA Ops:
  0.0 66.3 %main.1.in_ref = bf16[768,576]{1,0:T(8,128)(2,1)} custom-call(s32[32]{0:T(128)} %orient_ref.1, s32[32]{0:T(128)} %defocus_ref.1, s32[8]{0:T(128)} %tz_ref.1, s32[8]{0:T(128)} %tx_ref.1, bf16[32,48,768]{2,1,0:T(8,128)(2,1)} %image_ref.1, bf16[12,48,768]{2,1,0:T(8,128)(2,1)} %volume_ref.1, bf16[8,48,384]{2,1,0:T(8,128)(2,1)} %ctf_ref.1, ...), custom_call_target="tpu_custom_call" | custom-call | tf_op jit(solution)/shard_map/main/pallas_call | solution.py:465
  66.3 3.6 %zpass.1 = f32[2,576,384]{2,1,0:T(8,128)} custom-call(bf16[768,576]{1,0:T(8,128)(2,1)} %main.1.in_ref, bf16[768,768]{1,0:T(8,128)(2,1)} %constant.12.ztab_ref), custom_call_target="tpu_custom_call" | custom-call | tf_op jit(solution)/shard_map/zpass/pallas_call | solution.py:529

commit v5 on v4

--- a/solution.py
+++ b/solution.py
@@ -362,15 +362,19 @@
             x_tab[...], paired[:m, :], (((1,), (1,)), ((), ())), preferred_element_type=F32
         ).astype(BF16).reshape(NB, XL, m)
 
+    def batch_ends(c, src, dst):
+        if c in (0, CH + 1):
+            lanes = pl.ds(0, 256) if c == 0 else pl.ds(256, 128)
+            return along0.at[src, :, lanes], pieces0.at[dst, :, lanes]
+        return along1.at[c - 1, src], pieces1.at[c - 1, dst]
+
     def batch_piece(c, d):
         to = lax.rem(row_block + d, NB)
-        src = along0.at[to] if c == 0 else along1.at[c - 1, to]
-        dst = pieces0.at[row_block] if c == 0 else pieces1.at[c - 1, row_block]
+        src, dst = batch_ends(c, to, row_block)
         return batch_copy(src, dst, batch_send.at[c, d], batch_recv.at[c, d], to)
 
     def batch_local(c):
-        src = along0.at[row_block] if c == 0 else along1.at[c - 1, row_block]
-        dst = pieces0.at[row_block] if c == 0 else pieces1.at[c - 1, row_block]
+        src, dst = batch_ends(c, row_block, row_block)
         return pltpu.make_async_copy(src, dst, batch_own.at[c])
 
     def batch_go(c):
@@ -383,16 +387,20 @@
             batch_piece(c, d).wait()
         batch_local(c).wait()
 
-    along0[...] = update(0, 0, ZL)
+    along0[:, :, :256] = update(0, 0, 8)
     batch_go(0)
-    for o in range(5, ORI):
+    for o in range(5, 7):
         project(1, o)
+    forward_pieces(1)
+    project(1, 7)
     weigh(1)
-    forward_pieces(1)
     take_sums(1)
     for c in range(CH):
         along1[c] = update(1, c * ZC, (c + 1) * ZC)
         batch_go(c + 1)
+        if c == 1:
+            along0[:, :, 256:] = update(0, 8, ZL)
+            batch_go(CH + 1)
 
     loads[5].wait()
 
@@ -410,12 +418,15 @@
     targets = [(d, e) for d in range(15) for e in range(2)] + [(15, 0)]
     along_y[:, :, ZL * XL :] = jnp.zeros((NS, 2 * ZL, LANES - ZL * XL), BF16)
     wide0, wide1 = (2 * n for _, n in PARTS)
-    batch_done(0)
-    for z in range(ZL):
-        gathered[z * XL : (z + 1) * XL, : NB * wide0] = jnp.concatenate(
-            [pieces0[b, :, z * wide0 : (z + 1) * wide0] for b in range(NB)], axis=1
-        )
+    def take_first(low, high):
+        for z in range(low, high):
+            gathered[z * XL : (z + 1) * XL, : NB * wide0] = jnp.concatenate(
+                [pieces0[b, :, z * wide0 : (z + 1) * wide0] for b in range(NB)], axis=1
+            )
+
     for g, (first, last) in enumerate(GROUPS):
+        batch_done((0, CH + 1)[g])
+        take_first(first * ZC, last * ZC)
         for c in range(first, last):
             batch_done(c + 1)
             for zi in range(ZC):
@@ -500,7 +511,7 @@
             pltpu.VMEM((2 * BOX, ZL * XL), BF16),
             dma((6,)), dma((2,)), dma((2,)), dma((2, 15)), dma((2, 15)), dma((2, 15)), dma((2, 15)),
             dma((2, 16)), dma((2, 16)), dma((16,)), dma((16,)), dma((2,)), dma((2,)),
-            dma((CH + 1, NB)), dma((CH + 1, NB)), dma((CH + 1,)), dma((2, 32)), dma((2, 32)), dma((2,)), dma((2,)),
+            dma((CH + 2, NB)), dma((CH + 2, NB)), dma((CH + 2,)), dma((2, 32)), dma((2, 32)), dma((2,)), dma((2,)),
         ],
         compiler_params=pltpu.CompilerParams(vmem_limit_bytes=LIMIT, collective_id=0, has_side_effects=True),
         name="main",

time: 70.2 us -> 68.3 us (0.973)
  Pallas kernels: 69.9 us -> 68 us
    pallas_call x1, Pallas kernels: 66.3 us -> 64.4 us  [main(): pl.pallas_call(main_kernel, out_shape=jax.ShapeDtypeStruct((2 * BOX, ZL *...]
where the time goes in v5:
time: 68.3 us; the launch traced here: 68.2 us
  Pallas kernels  68 us (100%)
    pallas_call x1, Pallas kernels, main(): pl.pallas_call(main_kernel, out_shape=jax.ShapeDtypeStruct((2 * BOX, ZL *...  64.4 us
    pallas_call x1, Pallas kernels, zpass(): pl.pallas_call(zpass_kernel, out_shape=jax.ShapeDtypeStruct((2, ZL * XL,...  3.63 us

profile of v5, /device:TPU:1, one launch (start us, length us, event | category | flops | bytes accessed | tf_op | source)
XLA Modules:
  0.0 68.2 jit_solution(11650040926911002567)
XLA Ops:
  0.0 64.4 %main.1.in_ref = bf16[768,576]{1,0:T(8,128)(2,1)} custom-call(s32[32]{0:T(128)} %orient_ref.1, s32[32]{0:T(128)} %defocus_ref.1, s32[8]{0:T(128)} %tz_ref.1, s32[8]{0:T(128)} %tx_ref.1, bf16[32,48,768]{2,1,0:T(8,128)(2,1)} %image_ref.1, bf16[12,48,768]{2,1,0:T(8,128)(2,1)} %volume_ref.1, bf16[8,48,384]{2,1,0:T(8,128)(2,1)} %ctf_ref.1, ...), custom_call_target="tpu_custom_call" | custom-call | tf_op jit(solution)/shard_map/main/pallas_call | solution.py:476
  64.4 3.6 %zpass.1 = f32[2,576,384]{2,1,0:T(8,128)} custom-call(bf16[768,576]{1,0:T(8,128)(2,1)} %main.1.in_ref, bf16[768,768]{1,0:T(8,128)(2,1)} %constant.12.ztab_ref), custom_call_target="tpu_custom_call" | custom-call | tf_op jit(solution)/shard_map/zpass/pallas_call | solution.py:540
